TPU v7x, 256 devices: a whole 4x4x8 slice. The times are simulated.
256 devices in a mesh: dp: 32 (over y, x, core), tm: 8 (over z).
Axes of the slice: x: 4, y: 4, z: 8, core: 2. Of those that a mesh axis runs over, the one named last changes fastest.
Arguments:
- queries: bfloat16 [32, 16, 64, 3072], P('dp', 'tm'), may hold values from -16 to 16, as said below
- keys: bfloat16 [32, 16, 64, 3072], P('dp', 'tm'), may hold values from -6 to 6, as said below
- values: bfloat16 [32, 16, 64, 3072], P('dp', 'tm'), may hold values from -6 to 6
- out_grad: bfloat16 [32, 16, 64, 3072], P('dp', 'tm'), may hold values from -6 to 6
- action_table: float32 [8, 3072], replicated, may hold values from -6 to 6
- lam_tokens: bfloat16 [32, 16, 64, 1024], P('dp', 'tm'), may hold values from -60 to 60, as said below
- enc_weight: bfloat16 [1024, 1024], P('dp'), may hold values from -0.1875 to 0.1875
- codebook: float32 [8, 1024], replicated, may hold values from -6 to 6
- action_codes: int32 [32, 16], P('dp', 'tm'), may hold values from 0 to 7
- episode_start: int32 [32], P('dp'), may hold values from 0 to 15
Outputs:
- attn_out: bfloat16 [32, 16, 64, 3072], P('dp', 'tm')
- grad_q: bfloat16 [32, 16, 64, 3072], P('dp', 'tm')
- grad_k: bfloat16 [32, 16, 64, 3072], P('dp', 'tm')
- grad_v: bfloat16 [32, 16, 64, 3072], P('dp', 'tm')
- grad_actions: float32 [8, 3072], replicated
- grad_codebook: float32 [8, 1024], replicated
- grad_encoder: float32 [1024, 1024], P('dp')
Inputs may be any that keep to these rules, and one draw needn't show every extreme that they name: `queries`: bfloat16 activations. `keys`: bfloat16 activations. `lam_tokens`: bfloat16 tokens.
All inputs are finite; a program needn't handle non-finite values.
Results may differ from a plain program's by a relative error of at most 0.024.
Values may be sent and summed in bfloat16 or wider, within the bound.
A program may use at most 128 MiB of HBM per device.

v0:
```python
import math

import jax
import jax.numpy as jnp
from jax import lax
from jax.sharding import PartitionSpec as P

HS = 128
NC = 8


NEG_FILL = -1e30


def passed_along(shard, axis, by):
    peers = lax.axis_size(axis)
    pairs = [(i, i + by) for i in range(peers) if 0 <= i + by < peers]
    return lax.ppermute(shard, axis, pairs)


def frame_mask(query_frames, key_frames, per_frame, boundary):
    query_ids = jnp.arange(query_frames * per_frame, dtype=jnp.int32) // per_frame
    key_ids = jnp.arange(key_frames * per_frame, dtype=jnp.int32) // per_frame
    same_part = (key_ids[None, :] >= boundary) == (query_ids[:, None] >= boundary)
    return (key_ids[None, :] <= query_ids[:, None]) & same_part


def head_scores(query_heads, key_heads, visible):
    score_scale = 1.0 / math.sqrt(query_heads.shape[2])
    scores = (
        jnp.einsum("qhd,khd->hqk", query_heads, key_heads, preferred_element_type=jnp.float32)
        * score_scale
    )
    return jnp.where(visible[None], scores, NEG_FILL)


def forward_block(query_heads, key_heads, value_heads, visible):
    scores = head_scores(query_heads, key_heads, visible)
    row_top = jnp.max(scores, axis=2, keepdims=True)
    log_total = row_top + jnp.log(jnp.sum(jnp.exp(scores - row_top), axis=2, keepdims=True))
    weights = jnp.exp(scores - log_total).astype(jnp.bfloat16)
    output = jnp.einsum("hqk,khd->qhd", weights, value_heads, preferred_element_type=jnp.float32)
    return (output.astype(jnp.bfloat16), log_total)


def backward_block(query_heads, key_heads, value_heads, grad_heads, log_total, grad_dot, visible):
    score_scale = 1.0 / math.sqrt(query_heads.shape[2])
    scores = head_scores(query_heads, key_heads, visible)
    probability = jnp.exp(scores - log_total)
    prob_grad = jnp.einsum(
        "qhd,khd->hqk", grad_heads, value_heads, preferred_element_type=jnp.float32
    )
    score_grad = (probability * (prob_grad - grad_dot) * score_scale).astype(jnp.bfloat16)
    return (score_grad, probability.astype(jnp.bfloat16))


def inner_rows(grad_heads, out_heads):
    return jnp.einsum("qhd,qhd->hq", grad_heads, out_heads, preferred_element_type=jnp.float32)[
        :, :, None
    ]


def per_device(
    queries,
    keys,
    values,
    out_grad,
    action_table,
    lam_tokens,
    enc_weight,
    codebook,
    action_codes,
    episode_start,
):
    highest = lax.Precision.HIGHEST
    frames_here = queries.shape[1]
    per_frame = queries.shape[2]
    rows_here = frames_here * per_frame
    first_frame = lax.axis_index("tm") * frames_here
    boundary = episode_start[0]
    code_row = action_codes[0]
    onehot = (code_row[:, None] == jnp.arange(NC, dtype=jnp.int32)[None, :]).astype(jnp.float32)
    offsets = jnp.dot(onehot, action_table, precision=highest)
    conditioned = (queries[0].astype(jnp.float32) + offsets[:, None, :]).astype(jnp.bfloat16)
    keys_here = keys[0]
    values_here = values[0]
    grads_here = out_grad[0]
    query_split, key_split, value_split = (
        lax.all_to_all(conditioned, "tm", split_axis=2, concat_axis=0, tiled=True),
        lax.all_to_all(keys_here, "tm", split_axis=2, concat_axis=0, tiled=True),
        lax.all_to_all(values_here, "tm", split_axis=2, concat_axis=0, tiled=True),
    )
    all_frames = query_split.shape[0]
    local_width = query_split.shape[2]
    head_count = local_width // HS
    all_rows = all_frames * per_frame
    visible = frame_mask(all_frames, all_frames, per_frame, boundary)
    query_heads = query_split.reshape(all_rows, head_count, HS)
    key_heads = key_split.reshape(all_rows, head_count, HS)
    value_heads = value_split.reshape(all_rows, head_count, HS)
    out_heads, log_total = forward_block(query_heads, key_heads, value_heads, visible)
    attn_out = lax.all_to_all(
        out_heads.reshape(all_frames, per_frame, local_width),
        "tm",
        split_axis=0,
        concat_axis=2,
        tiled=True,
    )
    grad_split = lax.all_to_all(grads_here, "tm", split_axis=2, concat_axis=0, tiled=True)
    grad_heads = grad_split.reshape(all_rows, head_count, HS)
    grad_dot = inner_rows(grad_heads, out_heads)
    score_grad, weights = backward_block(
        query_heads, key_heads, value_heads, grad_heads, log_total, grad_dot, visible
    )
    split_shape = (all_frames, per_frame, local_width)
    query_part = jnp.einsum(
        "hqk,khd->qhd", score_grad, key_heads, preferred_element_type=jnp.float32
    ).astype(jnp.bfloat16)
    key_part = jnp.einsum(
        "hqk,qhd->khd", score_grad, query_heads, preferred_element_type=jnp.float32
    ).astype(jnp.bfloat16)
    value_part = jnp.einsum(
        "hqk,qhd->khd", weights, grad_heads, preferred_element_type=jnp.float32
    ).astype(jnp.bfloat16)
    grad_query, grad_key, grad_value = (
        lax.all_to_all(
            query_part.reshape(split_shape), "tm", split_axis=0, concat_axis=2, tiled=True
        ),
        lax.all_to_all(
            key_part.reshape(split_shape), "tm", split_axis=0, concat_axis=2, tiled=True
        ),
        lax.all_to_all(
            value_part.reshape(split_shape), "tm", split_axis=0, concat_axis=2, tiled=True
        ),
    )
    summed_grad = jnp.sum(grad_query.astype(jnp.float32), axis=1)
    action_term = jnp.dot(onehot.T, summed_grad, precision=highest)
    frames_in = lam_tokens[0]
    lam_width = frames_in.shape[2]
    last_frame = passed_along(frames_in[frames_here - 1 :], "tm", 1)
    previous = jnp.concatenate([last_frame, frames_in[: frames_here - 1]], axis=0)
    delta = (frames_in.astype(jnp.float32) - previous.astype(jnp.float32)).astype(jnp.bfloat16)
    delta_rows = delta.reshape(rows_here, lam_width)
    columns = delta_rows
    encoded = jnp.dot(
        columns,
        lax.all_gather(enc_weight, "dp", axis=0, tiled=True),
        preferred_element_type=jnp.float32,
    )
    pooled = jnp.mean(jax.nn.silu(encoded).reshape(frames_here, per_frame, lam_width), axis=1)
    target = jnp.dot(onehot, codebook, precision=highest)
    frame_ids = first_frame + jnp.arange(frames_here, dtype=jnp.int32)
    live_pairs = ((frame_ids >= 1) & (frame_ids != boundary)).astype(jnp.float32)
    total_frames = frames_here * lax.axis_size("tm")
    residual = (pooled - target) * live_pairs[:, None] / total_frames
    code_term = -jnp.dot(onehot.T, residual, precision=highest)
    sigmoid_u = jax.nn.sigmoid(encoded)
    silu_slope = (sigmoid_u * (1.0 + encoded * (1.0 - sigmoid_u))).reshape(
        frames_here, per_frame, lam_width
    )
    encoded_grad = (
        ((residual / per_frame)[:, None, :] * silu_slope)
        .astype(jnp.bfloat16)
        .reshape(rows_here, lam_width)
    )
    columns = delta_rows
    encoder_part = lax.psum_scatter(
        lax.dot_general(
            columns, encoded_grad, (((0,), (0,)), ((), ())), preferred_element_type=jnp.float32
        ).astype(jnp.bfloat16),
        "dp",
        scatter_dimension=0,
        tiled=True,
    )
    grad_encoder = lax.psum(encoder_part, "tm").astype(jnp.float32)
    grad_actions, grad_codebook = lax.psum((action_term, code_term), ("dp", "tm"))
    return (
        attn_out[None],
        grad_query[None],
        grad_key[None],
        grad_value[None],
        grad_actions,
        grad_codebook,
        grad_encoder,
    )


def solution(mesh):
    placed = (
        P("dp", "tm", None, None),
        P("dp", "tm", None, None),
        P("dp", "tm", None, None),
        P("dp", "tm", None, None),
        P(),
        P("dp", "tm", None, None),
        P("dp", None),
        P(),
        P("dp", "tm"),
        P("dp"),
    )
    return jax.shard_map(
        per_device,
        mesh=mesh,
        in_specs=placed,
        out_specs=(
            P("dp", "tm", None, None),
            P("dp", "tm", None, None),
            P("dp", "tm", None, None),
            P("dp", "tm", None, None),
            P(),
            P(),
            P("dp", None),
        ),
        check_vma=False,
    )
```

profile of v0, /device:TPU:2, one launch (start us, length us, event | category | flops | bytes accessed | tf_op | source)
XLA Modules:
  0.0 643.2 jit_solution(16513316114471038162)
XLA Ops:
  7.2 3.7 copy.68
  13.0 7.2 %fusion.40 = bf16[3072,2,64]{2,1,0:T(2,128)(2,1)S(1)} fusion(f32[2,3072]{0,1:T(8,128)S(1)} %fusion.29, bf16[1,2,64,3072]{2,1,3,0:T(2,128)(2,1)S(1)} %copy.68), kind=kLoop, calls=%fused_computation.72 | loop fusion | flops 1179648 | bytes 1597440
  22.2 8.5 %all-to-all-start = ((bf16[8,2,24576]{2,1,0:T(2,128)(2,1)}), bf16[8,2,24576]{2,1,0:T(2,128)(2,1)}, u32[]{:S(2)}, u32[]{:S(2)}) async-start(bf16[8,2,24576]{2,1,0:T(2,128)(2,1)} %reshape.221), calls=%async_computation | async-start | bytes 1572864 | tf_op jit(solution)/shard_map/all_to_all | solution.py:89
  37.4 16.5 %all-to-all-done = bf16[8,2,24576]{2,1,0:T(2,128)(2,1)} async-done(((bf16[8,2,24576]{2,1,0:T(2,128)(2,1)}), bf16[8,2,24576]{2,1,0:T(2,128)(2,1)}, u32[]{:S(2)}, u32[]{:S(2)}) %all-to-all-start) | async-done | bytes 786464 | tf_op jit(solution)/shard_map/all_to_all | solution.py:89
  53.8 4.2 all-to-all-start.1
  58.1 3.7 copy.75
  64.8 16.8 %all-to-all-done.1 = bf16[8,2,24576]{2,1,0:T(2,128)(2,1)} async-done(((bf16[8,2,24576]{2,1,0:T(2,128)(2,1)}), bf16[8,2,24576]{2,1,0:T(2,128)(2,1)}, u32[]{:S(2)}, u32[]{:S(2)}) %all-to-all-start.1) | async-done | bytes 786464 | tf_op jit(solution)/shard_map/all_to_all | solution.py:90
  81.7 4.2 all-to-all-start.2
  111.3 7.7 %all-to-all-start.4 = ((bf16[8,2,24576]{2,1,0:T(2,128)(2,1)}), bf16[8,2,24576]{2,1,0:T(2,128)(2,1)}, u32[]{:S(2)}, u32[]{:S(2)}) async-start(bf16[8,2,24576]{2,1,0:T(2,128)(2,1)} %reshape.225), calls=%async_computation.4 | async-start | bytes 1572864 | tf_op jit(solution)/shard_map/all_to_all | solution.py:109
  119.0 7.4 %fusion.1 = (f32[3,1024]{1,0:T(4,128)S(1)}, f32[3,1024,1024]{1,2,0:T(8,128)}) fusion(pred[1024,1024]{0,1:T(8,128)(4,1)S(1)} %compare_and_fusion, bf16[1024,3,128]{0,2,1:T(8,128)(2,1)} %copy.90, bf16[1024,3,128]{2,1,0:T(4,128)(2,1)S(1)} %reshape.204), kind=kOutput, calls=%fused_computation.5 | convolution fusion | flops 814740480 | bytes 15216640 | tf_op jit(solution)/shard_map/qhd,khd->hqk/dot_general | solution.py:31
  134.4 7.4 %exponential_reduce_fusion = f32[3,1024]{1,0:T(4,128)S(1)} fusion(f32[3,1024,1024]{1,2,0:T(8,128)} %get-tuple-element.11, f32[3,1024]{1,0:T(4,128)S(1)} %get-tuple-element.10, pred[1024,1024]{0,1:T(8,128)(4,1)S(1)} %compare_and_fusion), kind=kLoop, calls=%fused_computation.2 | loop fusion | flops 12579840 | bytes 13656064 | tf_op jit(solution)/shard_map/reduce_sum | solution.py:40
  149.4 9.8 %fusion.39 = (f32[3,1024,128]{2,1,0:T(8,128)S(1)}, bf16[3,1024,128]{2,1,0:T(8,128)(2,1)}) fusion(bf16[1024,3,128]{2,1,0:T(4,128)(2,1)} %reshape.205, f32[3,1024,1024]{1,2,0:T(8,128)} %get-tuple-element.11, f32[3,1024]{1,0:T(4,128)S(1)} %log_add_fusion, pred[1024,1024]{0,1:T(8,128)(4,1)S(1)} %compare_and_fusion), kind=kOutput, calls=%fused_computation.68 | convolution fusion | flops 818675712 | bytes 16789504 | tf_op jit(solution)/shard_map/hqk,khd->qhd/dot_general | solution.py:42
  160.8 8.1 %multiply_convert_fusion = bf16[3,1024,1024]{1,2,0:T(8,128)(2,1)S(1)} fusion(f32[3,1024,1024]{1,2,0:T(8,128)} %get-tuple-element.11, f32[3,1024]{1,0:T(4,128)S(1)} %copy.106, f32[3,1024]{1,0:T(4,128)S(1)} %log_add_fusion, pred[1024,1024]{0,1:T(8,128)(4,1)S(1)} %compare_and_fusion, bf16[1024,3,128]{2,1,0:T(4,128)(2,1)S(1)} %reshape.207, ...), kind=kOutput, calls=%fused_computation | convolution fusion | flops 827326464 | bytes 21520384 | tf_op jit(solution)/shard_map/qhd,khd->hqk/dot_general | solution.py:50
  176.1 7.0 %all-to-all-start.5 = ((bf16[16,64,384]{2,1,0:T(8,128)(2,1)}), bf16[16,64,384]{2,1,0:T(8,128)(2,1)S(1)}, u32[]{:S(2)}, u32[]{:S(2)}) async-start(bf16[16,64,384]{2,1,0:T(8,128)(2,1)} %reshape.208), calls=%async_computation.5 | async-start | bytes 1572864 | tf_op jit(solution)/shard_map/all_to_all | solution.py:126
  183.1 4.1 collective-permute-start
  187.3 14.6 %collective-permute-done = bf16[1,64,1024]{2,1,0:T(8,128)(2,1)S(1)} collective-permute-done((bf16[1,64,1024]{2,1,0:T(8,128)(2,1)S(1)}, bf16[1,64,1024]{2,1,0:T(8,128)(2,1)S(1)}, u32[]{:S(2)}, u32[]{:S(2)}) %collective-permute-start) | collective-permute-done | bytes 131104 | tf_op jit(solution)/shard_map/ppermute | solution.py:18
  202.8 6.1 fusion.4
  215.1 8.1 %all-to-all-start.6 = ((bf16[16,64,384]{2,1,0:T(8,128)(2,1)}), bf16[16,64,384]{2,1,0:T(8,128)(2,1)}, u32[]{:S(2)}, u32[]{:S(2)}) async-start(bf16[16,64,384]{2,1,0:T(8,128)(2,1)} %reshape.209), calls=%async_computation.6 | async-start | bytes 1572864 | tf_op jit(solution)/shard_map/all_to_all | solution.py:129
  226.8 7.8 %fusion.5 = bf16[1024,3,128]{2,0,1:T(8,128)(2,1)S(1)} fusion(bf16[1024,3,128]{2,1,0:T(4,128)(2,1)S(1)} %reshape.207, f32[3,1024,1024]{1,2,0:T(8,128)} %get-tuple-element.11, f32[3,1024]{1,0:T(4,128)S(1)} %log_add_fusion, pred[1024,1024]{0,1:T(8,128)(4,1)S(1)} %copy-done.4), kind=kOutput, calls=%fused_computation.18 | convolution fusion | flops 818282496 | bytes 15216640 | tf_op jit(solution)/shard_map/hqk,qhd->khd/dot_general | solution.py:122
  236.8 9.7 %all-to-all-done.6 = bf16[16,64,384]{2,1,0:T(8,128)(2,1)} async-done(((bf16[16,64,384]{2,1,0:T(8,128)(2,1)}), bf16[16,64,384]{2,1,0:T(8,128)(2,1)}, u32[]{:S(2)}, u32[]{:S(2)}) %all-to-all-start.6) | async-done | bytes 786464 | tf_op jit(solution)/shard_map/all_to_all | solution.py:129
  253.3 20.3 %all-to-all-done.7 = bf16[16,64,384]{2,1,0:T(8,128)(2,1)S(1)} async-done(((bf16[16,64,384]{2,1,0:T(8,128)(2,1)}), bf16[16,64,384]{2,1,0:T(8,128)(2,1)S(1)}, u32[]{:S(2)}, u32[]{:S(2)}) %all-to-all-start.7) | async-done | bytes 786464 | tf_op jit(solution)/shard_map/all_to_all | solution.py:132
  277.4 38.4 %reduce-scatter.2.cloned.1.call-done = bf16[32,1024]{1,0:T(8,128)(2,1)} async-done(((bf16[1024,1024]{1,0:T(8,128)(2,1)}), bf16[32,1024]{1,0:T(8,128)(2,1)}) %reduce-scatter.2.cloned.1.call-update) | async-done | bytes 65552 | tf_op jit(solution)/shard_map/reduce_scatter | solution.py:167
  325.2 73.8 %psum.22 = f32[8,1024]{1,0:T(8,128)} all-reduce(f32[8,1024]{1,0:T(8,128)S(1)} %convolution_negate_fusion), channel_id=1, replica_groups=mesh['dp'=32,'tm'=8] {'dp','tm'}, use_global_device_ids=true, to_apply=%region_5.6 | all-reduce | flops 8192 | bytes 65536 | tf_op jit(solution)/shard_map/psum | solution.py:176
  400.6 234.1 %all-reduce.3.cloned.1.call-done = f32[8,3072]{1,0:T(8,128)} async-done(((f32[8,3072]{1,0:T(8,128)}), f32[8,3072]{1,0:T(8,128)}) %all-reduce.3.cloned.1.call-update) | async-done | bytes 98320 | tf_op jit(solution)/shard_map/psum | solution.py:176
  (95 shorter events, 98.5 us)
Async XLA Ops:
  7.2 3.8 copy-start
  22.2 31.7 %all-to-all-start = ((bf16[8,2,24576]{2,1,0:T(2,128)(2,1)}), bf16[8,2,24576]{2,1,0:T(2,128)(2,1)}, u32[]{:S(2)}, u32[]{:S(2)}) async-start(bf16[8,2,24576]{2,1,0:T(2,128)(2,1)} %reshape.221), calls=%async_computation | async-start | bytes 1572864 | tf_op jit(solution)/shard_map/all_to_all | solution.py:89
  53.8 27.8 %all-to-all-start.1 = ((bf16[8,2,24576]{2,1,0:T(2,128)(2,1)}), bf16[8,2,24576]{2,1,0:T(2,128)(2,1)}, u32[]{:S(2)}, u32[]{:S(2)}) async-start(bf16[8,2,24576]{2,1,0:T(2,128)(2,1)} %reshape.223), calls=%async_computation.1 | async-start | bytes 1572864 | tf_op jit(solution)/shard_map/all_to_all | solution.py:90
  81.7 29.6 %all-to-all-start.2 = ((bf16[8,2,24576]{2,1,0:T(2,128)(2,1)}), bf16[8,2,24576]{2,1,0:T(2,128)(2,1)}, u32[]{:S(2)}, u32[]{:S(2)}) async-start(bf16[8,2,24576]{2,1,0:T(2,128)(2,1)} %reshape.219), calls=%async_computation.2 | async-start | bytes 1572864 | tf_op jit(solution)/shard_map/all_to_all | solution.py:91
  85.9 126.2 %all-gather.2.cloned.1.call-start = ((), (), s32[]{:S(2)}) async-start(), calls=%async_computation.10 | async-start | bytes 2162688 | tf_op jit(solution)/shard_map/all_gather | solution.py:147
  95.3 65.5 %copy-start.3 = (pred[1024,1024]{0,1:T(8,128)(4,1)}, pred[1024,1024]{0,1:T(8,128)(4,1)S(1)}, u32[]{:S(2)}) copy-start(pred[1024,1024]{0,1:T(8,128)(4,1)S(1)} %compare_and_fusion) | copy-start | bytes 3145732
  111.3 7.7 %copy-start.6 = (bf16[1024,3,128]{2,1,0:T(4,128)(2,1)}, bf16[1024,3,128]{2,1,0:T(4,128)(2,1)S(1)}, u32[]{:S(2)}) copy-start(bf16[1024,3,128]{2,1,0:T(4,128)(2,1)S(1)} %reshape.204) | copy-start | bytes 2359300
  111.3 30.7 %all-to-all-start.4 = ((bf16[8,2,24576]{2,1,0:T(2,128)(2,1)}), bf16[8,2,24576]{2,1,0:T(2,128)(2,1)}, u32[]{:S(2)}, u32[]{:S(2)}) async-start(bf16[8,2,24576]{2,1,0:T(2,128)(2,1)} %reshape.225), calls=%async_computation.4 | async-start | bytes 1572864 | tf_op jit(solution)/shard_map/all_to_all | solution.py:109
  160.8 10.7 %copy-start.7 = (bf16[1024,3,128]{2,1,0:T(4,128)(2,1)S(1)}, bf16[1024,3,128]{2,1,0:T(4,128)(2,1)}, u32[]{:S(2)}) copy-start(bf16[1024,3,128]{2,1,0:T(4,128)(2,1)} %copy-done.6) | copy-start | bytes 2359300
  168.9 2.6 copy-start.2
  171.5 11.6 %copy-start.5 = (bf16[1,2,64,1024]{3,2,1,0:T(8,128)(2,1)S(1)}, bf16[1,2,64,1024]{3,2,1,0:T(8,128)(2,1)}, u32[]{:S(2)}) copy-start(bf16[1,2,64,1024]{3,2,1,0:T(8,128)(2,1)} %param.15) | copy-start | bytes 786436
  176.1 39.0 %all-to-all-start.5 = ((bf16[16,64,384]{2,1,0:T(8,128)(2,1)}), bf16[16,64,384]{2,1,0:T(8,128)(2,1)S(1)}, u32[]{:S(2)}, u32[]{:S(2)}) async-start(bf16[16,64,384]{2,1,0:T(8,128)(2,1)} %reshape.208), calls=%async_computation.5 | async-start | bytes 1572864 | tf_op jit(solution)/shard_map/all_to_all | solution.py:126
  183.1 18.8 %collective-permute-start = (bf16[1,64,1024]{2,1,0:T(8,128)(2,1)S(1)}, bf16[1,64,1024]{2,1,0:T(8,128)(2,1)S(1)}, u32[]{:S(2)}, u32[]{:S(2)}) collective-permute-start(bf16[1,64,1024]{2,1,0:T(8,128)(2,1)S(1)} %get-tuple-element.9), channel_id=1, source_target_pairs={{0,1},{1,2},{2,3},{3,4},{4,5},{5,6},{6,7},{8,9},{9,10},{10,11},{11... | collective-permute-start | bytes 393224 | tf_op jit(solution)/shard_map/ppermute | solution.py:18
  208.9 14.3 %copy-start.8 = (s32[1,2]{1,0:T(1,128)S(1)}, s32[1,2]{1,0:T(1,128)}, u32[]{:S(2)}) copy-start(s32[1,2]{1,0:T(1,128)} %param.18) | copy-start | bytes 28
  208.9 14.3 %copy-start.9 = (f32[8,1024]{1,0:T(8,128)S(1)}, f32[8,1024]{1,0:T(8,128)}, u32[]{:S(2)}) copy-start(f32[8,1024]{1,0:T(8,128)} %param.17) | copy-start | bytes 98308
  212.0 14.8 %copy-start.4 = (pred[1024,1024]{0,1:T(8,128)(4,1)S(1)}, pred[1024,1024]{0,1:T(8,128)(4,1)}, u32[]{:S(2)}) copy-start(pred[1024,1024]{0,1:T(8,128)(4,1)} %copy-done.3) | copy-start | bytes 3145732
  215.1 31.4 %all-to-all-start.6 = ((bf16[16,64,384]{2,1,0:T(8,128)(2,1)}), bf16[16,64,384]{2,1,0:T(8,128)(2,1)}, u32[]{:S(2)}, u32[]{:S(2)}) async-start(bf16[16,64,384]{2,1,0:T(8,128)(2,1)} %reshape.209), calls=%async_computation.6 | async-start | bytes 1572864 | tf_op jit(solution)/shard_map/all_to_all | solution.py:129
  223.2 92.5 %reduce-scatter.2.cloned.1.call-start = ((), (), s32[]{:S(2)}) async-start(), calls=%async_computation.11 | async-start | bytes 2162688 | tf_op jit(solution)/shard_map/reduce_scatter | solution.py:167
  246.5 27.1 %all-to-all-start.7 = ((bf16[16,64,384]{2,1,0:T(8,128)(2,1)}), bf16[16,64,384]{2,1,0:T(8,128)(2,1)S(1)}, u32[]{:S(2)}, u32[]{:S(2)}) async-start(bf16[16,64,384]{2,1,0:T(8,128)(2,1)} %reshape.210), calls=%async_computation.7 | async-start | bytes 1572864 | tf_op jit(solution)/shard_map/all_to_all | solution.py:132
  273.6 49.6 %all-to-all-start.3 = ((bf16[16,64,384]{2,1,0:T(8,128)(2,1)}), bf16[16,64,384]{2,1,0:T(8,128)(2,1)S(1)}, u32[]{:S(2)}, u32[]{:S(2)}) async-start(bf16[16,64,384]{2,1,0:T(8,128)(2,1)} %reshape.206), calls=%async_computation.3 | async-start | bytes 1572864 | tf_op jit(solution)/shard_map/all_to_all | solution.py:102
  277.1 121.9 %all-reduce.5.cloned.1.call-start = ((), (), s32[]{:S(2)}) async-start(), calls=%async_computation.12 | async-start | bytes 131072 | tf_op jit(solution)/shard_map/psum | solution.py:175
  315.8 318.9 %all-reduce.3.cloned.1.call-start = ((), (), s32[]{:S(2)}) async-start(), calls=%async_computation.9 | async-start | bytes 196608 | tf_op jit(solution)/shard_map/psum | solution.py:176
  317.0 319.2 %copy-start.1 = (f32[8,3072]{1,0:T(8,128)S(1)}, f32[8,3072]{1,0:T(8,128)}, u32[]{:S(2)}) copy-start(f32[8,3072]{1,0:T(8,128)} %param.14) | copy-start | bytes 294916
Sparse Core Ops, SparseCore 0:
  89.3 49.9 all-gather.1
  227.9 87.8 reduce-scatter.1
  318.0 70.9 all-reduce.4
  395.9 238.6 all-reduce.2
where the time goes:
time: 654 us; the launch traced here: 643 us
  waiting for transfers between devices  351 us (54%)
  local copies, waits for them, and re-layouts  80.1 us (12%)
  blocking collectives  73.8 us (11%)
  starting transfers between devices  51.4 us (8%)
  matrix products  50.3 us (8%)
  other arithmetic  21 us (3%)
  between operations  15.2 us (2%)
    psum x1, waiting for transfers between devices, per_device(): lax.psum((action_term, code_term), ('dp', 'tm'))  234 us
    psum x1, blocking collectives, per_device(): lax.psum((action_term, code_term), ('dp', 'tm'))  73.8 us
    unnamed x36, local copies, waits for them, and re-layouts  39 us
    reduce_scatter x1, waiting for transfers between devices, per_device(): lax.psum_scatter(lax.dot_general(columns, encoded_grad, (((0,), (0,)), ((...  38.4 us
    all_to_all x1, waiting for transfers between devices, per_device(): lax.all_to_all(value_part.reshape(split_shape), 'tm', split_axis=0, conca...  20.3 us
    all_to_all x1, waiting for transfers between devices, per_device(): lax.all_to_all(keys_here, 'tm', split_axis=2, concat_axis=0, tiled=True)  16.8 us
    all_to_all x1, waiting for transfers between devices, per_device(): lax.all_to_all(conditioned, 'tm', split_axis=2, concat_axis=0, tiled=True)  16.5 us
    ppermute x1, waiting for transfers between devices, passed_along(): return lax.ppermute(shard, axis, pairs)  14.6 us
  transfers between devices with their start and end apart: 13, of which 8 were waited for; matrix products, arithmetic and copies ran while one was open for 21% of the time, Pallas kernels for 0%

commit v1 on v0

v1 whole, which is shorter than its diff:
```python
import functools
import math

import jax
import jax.numpy as jnp
from jax import lax
from jax.experimental import pallas as pl
from jax.experimental.pallas import tpu as pltpu
from jax.sharding import PartitionSpec as P

HS = 128
NC = 8
NEG_FILL = -1e30
MESH = pl.DeviceIdType.MESH
BF = jnp.bfloat16
F32 = jnp.float32


def dot(a, b):
    return jnp.dot(a, b, preferred_element_type=F32)


def wait_bytes(view, sem):
    pltpu.make_async_copy(view, view, sem).wait()


def kernel(
    sizes,
    q_ref, k_ref, v_ref, g_ref, tab_ref, lam_ref, enc_ref, book_ref, code_ref, start_ref,
    o_out, dq_out, dk_out, dv_out, ga_out, gc_out, ge_out,
    cond, qb, kb, vb, gb, ob, dqb, dkb, dvb, kt, vt, qt, gt, dk_acc, dv_acc,
    onehot, prev, wg, dw, rc, s1, ry, s2, rx, s3, rt, s4,
    cterm, cin, blob, core_in, y_in, x_in,
    in_recv, in_send, out_recv, out_send, small_recv, small_send,
):
    ny, nx, nc, nt, chunk = sizes
    heads = qb.shape[0]
    rows = qb.shape[1]
    here = rows // nt
    per_frame = here // 2
    width = heads * HS
    lam_width = lam_ref.shape[1]
    part = lam_width // nt
    enc_rows = enc_ref.shape[0]
    dp = lax.axis_index("dp")
    me = lax.axis_index("tm")
    core = dp % nc
    xx = (dp // nc) % nx
    yy = dp // (nc * nx)

    def at_t(t):
        return (dp, t)

    def at_x(x):
        return ((yy * nx + x) * nc + core, me)

    def at_y(y):
        return ((y * nx + xx) * nc + core, me)

    other_core = ((yy * nx + xx) * nc + (nc - 1 - core), me)

    def over_t(fn):
        def body(i, carry):
            step = nt // 2 + (1 - 2 * (i % 2)) * ((i + 1) // 2)
            fn((me + step) % nt)
            return carry

        lax.fori_loop(0, nt - 1, body, 0)

    def over_x(fn):
        def body(i, carry):
            fn((xx + 1 + i) % nx)
            return carry

        lax.fori_loop(0, nx - 1, body, 0)

    def over_y(fn):
        def body(i, carry):
            fn((yy + 1 + i) % ny)
            return carry

        lax.fori_loop(0, ny - 1, body, 0)

    barrier = pltpu.get_barrier_semaphore()

    def greet(device):
        pl.semaphore_signal(barrier, inc=1, device_id=device, device_id_type=MESH)

    over_t(lambda t: greet(at_t(t)))
    over_x(lambda x: greet(at_x(x)))
    over_y(lambda y: greet(at_y(y)))
    greet(other_core)
    pl.semaphore_wait(barrier, (nt - 1) + (nx - 1) + (ny - 1) + 1)

    def send(src, dst, sem_s, sem_r, device):
        pltpu.make_async_remote_copy(
            src_ref=src, dst_ref=dst, send_sem=sem_s, recv_sem=sem_r,
            device_id=device, device_id_type=MESH,
        ).start()

    LAM, AGX, AGY, AGC, HOT, RSC, RSY, RSX, RST, GE, CT, ARC, ARY, ARX, FA, FC = range(16)

    def small(src, dst, index, device):
        send(src, dst, small_send.at[index], small_recv.at[index], device)

    def lanes(index, size):
        return pl.ds(pl.multiple_of(index * size, size), size)

    wg[yy, xx, core] = enc_ref[...]
    over_x(lambda x: small(enc_ref, wg.at[yy, xx, core], AGX, at_x(x)))
    small(lam_ref.at[pl.ds(per_frame, per_frame)], prev, LAM, at_t((me + 1) % nt))
    code_a, code_b = code_ref[0, 0], code_ref[0, 1]
    boundary = start_ref[0]
    lane_code = jnp.where(
        lax.broadcasted_iota(jnp.int32, (NC, here), 1) < per_frame, code_a, code_b
    )
    hot_here = (lax.broadcasted_iota(jnp.int32, (NC, here), 0) == lane_code).astype(F32)
    onehot[:, lanes(me, here)] = hot_here
    over_t(lambda t: small(onehot.at[:, lanes(me, here)], onehot.at[:, lanes(me, here)], HOT, at_t(t)))

    mine = pl.ds(pl.multiple_of(me * here, here), here)

    def scatter_in(index, src, dst, head):
        def one(t):
            send(
                src.at[:, lanes(t * heads + head, HS)], dst.at[head, mine],
                in_send.at[index], in_recv.at[index, head], at_t(t),
            )

        over_t(one)
        pltpu.make_async_copy(
            src.at[:, lanes(me * heads + head, HS)], dst.at[head, mine], in_recv.at[index, head]
        ).start()

    scatter_in(1, k_ref, kb, 0)
    scatter_in(2, v_ref, vb, 0)
    table = tab_ref[...]
    code_ids = lax.broadcasted_iota(jnp.int32, table.shape, 0)
    for frame, code in ((0, code_a), (1, code_b)):
        offset = jnp.sum(jnp.where(code_ids == code, table, 0.0), axis=0, keepdims=True)
        span = pl.ds(frame * per_frame, per_frame)
        cond[span] = (q_ref[span].astype(F32) + offset).astype(BF)
    scatter_in(0, cond, qb, 0)
    scatter_in(3, g_ref, gb, 0)
    for head in range(1, heads):
        scatter_in(1, k_ref, kb, head)
        scatter_in(0, cond, qb, head)
        scatter_in(2, v_ref, vb, head)
        scatter_in(3, g_ref, gb, head)

    wait_bytes(wg.at[0, pl.ds(0, nx - 1), 0], small_recv.at[AGX])
    over_y(lambda y: small(wg.at[yy, :, core], wg.at[yy, :, core], AGY, at_y(y)))
    wait_bytes(prev, small_recv.at[LAM])
    lam = lam_ref[...].astype(F32)
    before = jnp.where(me > 0, prev[...].astype(F32), 0.0)
    delta = jnp.concatenate(
        [lam[:per_frame] - before, lam[per_frame:] - lam[:per_frame]], axis=0
    ).astype(BF)
    wait_bytes(wg.at[pl.ds(0, ny - 1), :, 0], small_recv.at[AGY])
    small(wg.at[:, :, core], wg.at[:, :, core], AGC, other_core)
    delta_t = delta.T
    wait_bytes(wg.at[:, :, 0], small_recv.at[AGC])
    slab = lam_width // ny
    encoded = jnp.zeros((here, lam_width), F32)
    for y in range(ny):
        encoded += dot(delta[:, y * slab:(y + 1) * slab], wg[y].reshape(slab, lam_width))
    sig = jax.nn.sigmoid(encoded)
    act = encoded * sig
    slope = sig * (1.0 + encoded * (1.0 - sig))
    book = book_ref[...]
    book_ids = lax.broadcasted_iota(jnp.int32, book.shape, 0)
    term = jnp.zeros(book.shape, F32)
    graded = []
    for frame, code in ((0, code_a), (1, code_b)):
        span = slice(frame * per_frame, (frame + 1) * per_frame)
        pooled = jnp.sum(act[span], axis=0, keepdims=True) * (1.0 / per_frame)
        target = jnp.sum(jnp.where(book_ids == code, book, 0.0), axis=0, keepdims=True)
        frame_id = me * 2 + frame
        live = jnp.where((frame_id >= 1) & (frame_id != boundary), 1.0 / (2 * nt), 0.0)
        residual = (pooled - target) * live
        term -= jnp.where(book_ids == code, residual, 0.0)
        graded.append(residual * (1.0 / per_frame) * slope[span])
    encoded_grad = jnp.concatenate(graded, axis=0).astype(BF)
    for t in range(nt):
        cterm[t] = term[:, t * part:(t + 1) * part]
    cin[me] = cterm[me]
    over_t(lambda t: small(cterm.at[t], cin.at[me], CT, at_t(t)))
    for yx in range(ny * nx):
        lo = yx * nc * enc_rows
        piece = dot(delta_t[lo:lo + nc * enc_rows], encoded_grad).astype(BF)
        for c in range(nc):
            dw[c, yx // nx, yx % nx] = piece[c * enc_rows:(c + 1) * enc_rows]
    small(dw.at[nc - 1 - core], rc, RSC, other_core)

    def add_cores():
        wait_bytes(rc, small_recv.at[RSC])
        for y in range(ny):
            s1[y] = (dw[core, y].astype(F32) + rc[y].astype(F32)).astype(BF)
        over_y(lambda y: small(s1.at[y], ry.at[yy], RSY, at_y(y)))
        ry[yy] = s1[yy]

    def add_y():
        wait_bytes(ry.at[pl.ds(0, ny - 1)], small_recv.at[RSY])
        total = ry[0].astype(F32)
        for y in range(1, ny):
            total += ry[y].astype(F32)
        s2[...] = total.astype(BF)
        over_x(lambda x: small(s2.at[x], rx.at[xx], RSX, at_x(x)))
        rx[xx] = s2[xx]

    def add_x():
        wait_bytes(rx.at[pl.ds(0, nx - 1)], small_recv.at[RSX])
        total = rx[0].astype(F32)
        for x in range(1, nx):
            total += rx[x].astype(F32)
        total = total.astype(BF)
        for t in range(nt):
            s3[t] = total[:, t * part:(t + 1) * part]
        over_t(lambda t: small(s3.at[t], rt.at[me], RST, at_t(t)))
        rt[me] = s3[me]

    def add_t():
        wait_bytes(rt.at[pl.ds(0, nt - 1)], small_recv.at[RST])
        total = rt[0].astype(F32)
        for t in range(1, nt):
            total += rt[t].astype(F32)
        s4[...] = total.astype(BF).astype(F32)
        over_t(lambda t: small(s4, ge_out.at[:, lanes(me, part)], GE, at_t(t)))
        pltpu.make_async_copy(s4, ge_out.at[:, lanes(me, part)], small_recv.at[GE]).start()

    score_scale = 1.0 / math.sqrt(HS)
    exp_scale = score_scale * math.log2(math.e)

    def attend(head):
        for index, block in ((0, qb), (1, kb), (2, vb), (3, gb)):
            wait_bytes(block.at[head], in_recv.at[index, head])
        kt[...] = kb[head].T
        vt[...] = vb[head].T
        qt[...] = qb[head].T
        gt[...] = gb[head].T
        for c in reversed(range(rows // chunk)):
            size = (c + 1) * chunk
            span = slice(c * chunk, size)
            scores = dot(kb[head, :size], qt[:, span])
            frame_of = (lax.broadcasted_iota(jnp.int32, (1, chunk), 1) + c * chunk) // per_frame
            low = jnp.where(frame_of >= boundary, boundary, 0) * per_frame
            high = (frame_of + 1) * per_frame
            key_ids = lax.broadcasted_iota(jnp.int32, (size, chunk), 0)
            scores = jnp.where((key_ids >= low) & (key_ids < high), scores, NEG_FILL)
            top = jnp.max(scores, axis=0, keepdims=True)
            prob = jnp.exp2((scores - top) * exp_scale)
            prob = prob * (1.0 / jnp.sum(prob, axis=0, keepdims=True))
            weights = prob.astype(BF)
            out_t = dot(vt[:, :size], weights).astype(BF)
            ob[head, span] = out_t.T
            g_t = gt[:, span]
            grad_dot = jnp.sum(g_t.astype(F32) * out_t.astype(F32), axis=0, keepdims=True)
            prob_grad = dot(vb[head, :size], g_t)
            score_grad = (prob * ((prob_grad - grad_dot) * score_scale)).astype(BF)
            dqb[head, span] = dot(kt[:, :size], score_grad).astype(BF).T
            dk_part = dot(score_grad, qb[head, span])
            dv_part = dot(weights, gb[head, span])
            if size == rows:
                dk_acc[...] = dk_part
                dv_acc[...] = dv_part
            else:
                dk_acc[:size] += dk_part
                dv_acc[:size] += dv_part
        dkb[head] = dk_acc[...].astype(BF)
        dvb[head] = dv_acc[...].astype(BF)
        for index, src, dst in ((0, ob, o_out), (1, dqb, dq_out), (2, dkb, dk_out), (3, dvb, dv_out)):
            columns = lanes(me * heads + head, HS)

            def block(t):
                return src.at[head, pl.ds(pl.multiple_of(t * here, here), here)]

            over_t(lambda t: send(
                block(t), dst.at[:, columns], out_send.at[index], out_recv.at[index], at_t(t)
            ))
            pltpu.make_async_copy(block(me), dst.at[:, columns], out_recv.at[index]).start()

    def head_step(head, carry):
        attend(head)

        @pl.when(head == 0)
        def _():
            add_cores()

        @pl.when(head == 1)
        def _():
            add_y()

        return carry

    lax.fori_loop(0, heads, head_step, 0)
    add_x()

    wait_bytes(onehot.at[:, pl.ds(0, (nt - 1) * here)], small_recv.at[HOT])
    hot = onehot[...].astype(BF)
    for head in range(heads):
        blob[:, head * HS:(head + 1) * HS] = dot(hot, dqb[head])
    wait_bytes(cin.at[pl.ds(0, nt - 1)], small_recv.at[CT])
    total = cin[0]
    for t in range(1, nt):
        total += cin[t]
    blob[:, width:] = total
    small(blob, core_in, ARC, other_core)
    add_t()
    wait_bytes(core_in, small_recv.at[ARC])
    y_in[yy] = blob[...] + core_in[...]
    over_y(lambda y: small(y_in.at[yy], y_in.at[yy], ARY, at_y(y)))
    wait_bytes(y_in.at[pl.ds(0, ny - 1)], small_recv.at[ARY])
    total = y_in[0]
    for y in range(1, ny):
        total += y_in[y]
    x_in[xx] = total
    over_x(lambda x: small(x_in.at[xx], x_in.at[xx], ARX, at_x(x)))
    wait_bytes(x_in.at[pl.ds(0, nx - 1)], small_recv.at[ARX])
    total = x_in[0]
    for x in range(1, nx):
        total += x_in[x]
    wait_bytes(blob, small_send.at[ARC])
    blob[...] = total
    act_part, book_part = blob.at[:, pl.ds(0, width)], blob.at[:, pl.ds(width, part)]
    act_dst, book_dst = ga_out.at[:, lanes(me, width)], gc_out.at[:, lanes(me, part)]
    over_t(lambda t: small(act_part, act_dst, FA, at_t(t)))
    over_t(lambda t: small(book_part, book_dst, FC, at_t(t)))
    pltpu.make_async_copy(act_part, act_dst, small_recv.at[FA]).start()
    pltpu.make_async_copy(book_part, book_dst, small_recv.at[FC]).start()

    for index, dst in enumerate((o_out, dq_out, dk_out, dv_out)):
        wait_bytes(dst, out_recv.at[index])
    wait_bytes(ge_out, small_recv.at[GE])
    wait_bytes(ga_out, small_recv.at[FA])
    wait_bytes(gc_out, small_recv.at[FC])
    sent = qb.at[:, pl.ds(0, rows - here)]
    for index in range(4):
        wait_bytes(sent, in_send.at[index])
        wait_bytes(sent, out_send.at[index])
    for index, view in (
        (LAM, prev),
        (AGX, wg.at[0, pl.ds(0, nx - 1), 0]),
        (AGY, wg.at[pl.ds(0, ny - 1), :, 0]),
        (AGC, wg.at[:, :, 0]),
        (HOT, onehot.at[:, pl.ds(0, (nt - 1) * here)]),
        (RSC, rc),
        (RSY, ry.at[pl.ds(0, ny - 1)]),
        (RSX, rx.at[pl.ds(0, nx - 1)]),
        (RST, rt.at[pl.ds(0, nt - 1)]),
        (GE, ge_out.at[:, pl.ds(0, (nt - 1) * part)]),
        (CT, cin.at[pl.ds(0, nt - 1)]),
        (ARY, y_in.at[pl.ds(0, ny - 1)]),
        (ARX, x_in.at[pl.ds(0, nx - 1)]),
        (FA, ga_out.at[:, pl.ds(0, (nt - 1) * width)]),
        (FC, gc_out.at[:, pl.ds(0, (nt - 1) * part)]),
    ):
        wait_bytes(view, small_send.at[index])


def per_device(
    ny, nx, nc, nt, chunk,
    queries, keys, values, out_grad, action_table, lam_tokens, enc_weight, codebook,
    action_codes, episode_start,
):
    shape = queries.shape
    here = shape[1] * shape[2]
    wide = shape[3]
    lam_width = lam_tokens.shape[3]
    heads = wide // HS // nt
    rows = here * nt
    part = lam_width // nt
    enc_rows = enc_weight.shape[0]
    vmem = pl.BlockSpec(memory_space=pltpu.VMEM)
    smem = pl.BlockSpec(memory_space=pltpu.SMEM)
    anywhere = pl.BlockSpec(memory_space=pl.ANY)
    head_block = pltpu.VMEM((heads, rows, HS), BF)
    turned = pltpu.VMEM((HS, rows), BF)
    flops = heads * rows * rows * HS * 2 * 6 + 2 * 2 * here * lam_width * lam_width
    flat = jax.ShapeDtypeStruct((here, wide), BF)
    results = pl.pallas_call(
        functools.partial(kernel, (ny, nx, nc, nt, chunk)),
        out_shape=(
            flat, flat, flat, flat,
            jax.ShapeDtypeStruct(action_table.shape, F32),
            jax.ShapeDtypeStruct(codebook.shape, F32),
            jax.ShapeDtypeStruct(enc_weight.shape, F32),
        ),
        in_specs=[vmem, anywhere, anywhere, anywhere, vmem, vmem, vmem, vmem, smem, smem],
        out_specs=[anywhere] * 7,
        scratch_shapes=[
            pltpu.VMEM((here, wide), BF),
            head_block, head_block, head_block, head_block,
            head_block, head_block, head_block, head_block,
            turned, turned, turned, turned,
            pltpu.VMEM((rows, HS), F32),
            pltpu.VMEM((rows, HS), F32),
            pltpu.VMEM((NC, rows), F32),
            pltpu.VMEM((here // 2, lam_width), BF),
            pltpu.VMEM((ny, nx, nc, enc_rows, lam_width), BF),
            pltpu.VMEM((nc, ny, nx, enc_rows, lam_width), BF),
            pltpu.VMEM((ny, nx, enc_rows, lam_width), BF),
            pltpu.VMEM((ny, nx, enc_rows, lam_width), BF),
            pltpu.VMEM((ny, nx, enc_rows, lam_width), BF),
            pltpu.VMEM((nx, enc_rows, lam_width), BF),
            pltpu.VMEM((nx, enc_rows, lam_width), BF),
            pltpu.VMEM((nt, enc_rows, part), BF),
            pltpu.VMEM((nt, enc_rows, part), BF),
            pltpu.VMEM((enc_rows, part), F32),
            pltpu.VMEM((nt, NC, part), F32),
            pltpu.VMEM((nt, NC, part), F32),
            pltpu.VMEM((NC, heads * HS + part), F32),
            pltpu.VMEM((NC, heads * HS + part), F32),
            pltpu.VMEM((ny, NC, heads * HS + part), F32),
            pltpu.VMEM((nx, NC, heads * HS + part), F32),
            pltpu.SemaphoreType.DMA((4, heads)),
            pltpu.SemaphoreType.DMA((4,)),
            pltpu.SemaphoreType.DMA((4,)),
            pltpu.SemaphoreType.DMA((4,)),
            pltpu.SemaphoreType.DMA((16,)),
            pltpu.SemaphoreType.DMA((16,)),
        ],
        compiler_params=pltpu.CompilerParams(
            collective_id=0, has_side_effects=True, vmem_limit_bytes=56 * 2**20
        ),
        cost_estimate=pl.CostEstimate(
            flops=flops, bytes_accessed=8 * here * wide * 2, transcendentals=heads * rows * rows
        ),
    )(
        queries.reshape(here, wide), keys.reshape(here, wide), values.reshape(here, wide),
        out_grad.reshape(here, wide), action_table, lam_tokens.reshape(here, lam_width),
        enc_weight, codebook, action_codes, episode_start,
    )
    return tuple(r.reshape(shape) for r in results[:4]) + tuple(results[4:])


def solution(mesh, dims=(4, 4, 2), chunk=256):
    ny, nx, nc = dims
    nt = mesh.shape["tm"]
    frames = P("dp", "tm", None, None)
    return jax.shard_map(
        functools.partial(per_device, ny, nx, nc, nt, chunk),
        mesh=mesh,
        in_specs=(
            frames, frames, frames, frames, P(), frames, P("dp", None), P(), P("dp", "tm"), P("dp"),
        ),
        out_specs=(frames, frames, frames, frames, P(), P(), P("dp", None)),
        check_vma=False,
    )
```

time: 654 us -> 177 us (0.27); the launches traced: 643 us -> 177 us
  waiting for transfers between devices: 351 us -> 0 us
  Pallas kernels: 0 us -> 167 us
  blocking collectives: 73.8 us -> 0 us
  local copies, waits for them, and re-layouts: 80.1 us -> 7.96 us
  starting transfers between devices: 51.4 us -> 0 us
  matrix products: 50.3 us -> 0 us
  other arithmetic: 21 us -> 0 us
  between operations: 15.2 us -> 1.31 us
    psum x2 -> x0, waiting for transfers between devices: 234 us -> none  [the longest x1 234 us: per_device(): lax.psum((action_term, code_term), ('dp', 'tm'))]
    pallas_call x0 -> x1, Pallas kernels: none -> 167 us  [per_device(): pl.pallas_call(functools.partial(kernel, (ny, nx, nc, nt, chunk)), out_sh...]
    psum x1 -> x0, blocking collectives: 73.8 us -> none  [per_device(): lax.psum((action_term, code_term), ('dp', 'tm'))]
    all_to_all x8 -> x0, waiting for transfers between devices: 63.5 us -> none  [the longest x1 20.3 us: per_device(): lax.all_to_all(value_part.reshape(split_shape), 'tm', split_axis=0, conca...]
    dot_general x12 -> x0, matrix products: 50.3 us -> none  [the longest x1 9.83 us: forward_block(): jnp.einsum('hqk,khd->qhd', weights, value_heads, preferred_element_type=j...]
    all_to_all x8 -> x0, starting transfers between devices: 46.8 us -> none  [the longest x1 8.47 us: per_device(): lax.all_to_all(conditioned, 'tm', split_axis=2, concat_axis=0, tiled=True)]
    reduce_scatter x1 -> x0, waiting for transfers between devices: 38.4 us -> none  [per_device(): lax.psum_scatter(lax.dot_general(columns, encoded_grad, (((0,), (0,)), ((...]
    unnamed x36 -> x19, local copies, waits for them, and re-layouts: 39 us -> 7.96 us
  transfers between devices with their start and end apart: 13 -> 0, of which waited for: 8 -> 0; matrix products, arithmetic and copies ran while one was open for 21% -> 0% of each run, Pallas kernels for 0% -> 0%
where the time goes in v1:
time: 177 us
  Pallas kernels  167 us (94%)
  local copies, waits for them, and re-layouts  7.96 us (4%)
    pallas_call x1, Pallas kernels, per_device(): pl.pallas_call(functools.partial(kernel, (ny, nx, nc, nt, chunk)), out_sh...  167 us
    unnamed x19, local copies, waits for them, and re-layouts  7.96 us

profile of v1, /device:TPU:2, one launch (start us, length us, event | category | flops | bytes accessed | tf_op | source)
XLA Modules:
  0.0 176.7 jit_solution(6397632425544653733)
XLA Ops:
  1.3 167.4 %shard_map.153 = (bf16[128,3072]{1,0:T(8,128)(2,1)}, bf16[128,3072]{1,0:T(8,128)(2,1)}, bf16[128,3072]{1,0:T(8,128)(2,1)}, bf16[128,3072]{1,0:T(8,128)(2,1)}, f3...) custom-call(bf16[128,3072]{1,0:T(8,128)(2,1)} %bitcast.13, bf16[128,3072]{1,0:T(8,128)(2,1)} %bitcast.14, ...), custom_call_target="tpu_custom_call" | custom-call | flops 5368709120 | bytes 6291456 | tf_op jit(solution)/shard_map/pallas_call | solution.py:380
  168.7 0.0 copy-start.2
  168.7 2.1 %copy.25 = bf16[1,2,64,3072]{3,2,1,0:T(8,128)(2,1)} copy(bf16[1,2,64,3072]{3,2,1,0:T(8,128)(2,1)} %bitcast.12) | data formatting | bytes 1572864
  170.8 0.0 copy-done.2
  170.8 0.0 copy-start.1
  170.8 0.9 copy.26
  171.7 0.5 copy-done.1
  172.3 0.0 copy-start
  172.3 0.9 copy.27
  173.1 0.5 copy-done
  173.7 0.0 copy-start.4
  173.7 0.9 copy.28
  174.6 0.1 copy-done.4
  174.6 0.0 copy-start.5
  174.6 0.0 copy-start.3
  174.6 0.6 copy.29
  175.3 0.1 copy-done.5
  175.4 0.6 copy.30
  176.0 0.0 copy-done.3
  176.0 0.7 copy.31
Async XLA Ops:
  168.7 2.1 %copy-start.2 = (bf16[128,3072]{1,0:T(8,128)(2,1)S(1)}, bf16[128,3072]{1,0:T(8,128)(2,1)}, u32[]{:S(2)}) copy-start(bf16[128,3072]{1,0:T(8,128)(2,1)} %get-tuple-element.15) | copy-start | bytes 2359300
  170.8 1.4 copy-start.1
  172.3 1.4 copy-start
  173.7 1.0 copy-start.4
  174.6 0.8 copy-start.5
  174.6 1.4 copy-start.3

commit v2 on v1

--- a/solution.py
+++ b/solution.py
@@ -26,12 +26,12 @@
 
 def kernel(
     sizes,
-    q_ref, k_ref, v_ref, g_ref, tab_ref, lam_ref, enc_ref, book_ref, code_ref, start_ref,
+    q_hbm, k_ref, v_ref, g_ref, tab_hbm, lam_hbm, enc_hbm, book_hbm, code_ref, start_ref,
     o_out, dq_out, dk_out, dv_out, ga_out, gc_out, ge_out,
-    cond, qb, kb, vb, gb, ob, dqb, dkb, dvb, kt, vt, qt, gt, dk_acc, dv_acc,
-    onehot, prev, wg, dw, rc, s1, ry, s2, rx, s3, rt, s4,
+    q_ref, tab_ref, lam_ref, book_ref, cond, qb, kb, vb, gb, ob, dqb, dkb, dvb, kt, vt, qt, gt, dk_acc, dv_acc,
+    onehot, prev, wg, dw, rc, s1, ry, s2, rx, s3, rt, s4, ge,
     cterm, cin, blob, core_in, y_in, x_in,
-    in_recv, in_send, out_recv, out_send, small_recv, small_send,
+    load, in_recv, in_send, out_recv, out_send, small_recv, small_send,
 ):
     ny, nx, nc, nt, chunk = sizes
     heads = qb.shape[0]
@@ -41,7 +41,7 @@
     width = heads * HS
     lam_width = lam_ref.shape[1]
     part = lam_width // nt
-    enc_rows = enc_ref.shape[0]
+    enc_rows = enc_hbm.shape[0]
     dp = lax.axis_index("dp")
     me = lax.axis_index("tm")
     core = dp % nc
@@ -81,6 +81,17 @@
 
         lax.fori_loop(0, ny - 1, body, 0)
 
+    own_rows = wg.at[yy, xx, core]
+    loads = [
+        pltpu.make_async_copy(src, dst, load.at[i])
+        for i, (src, dst) in enumerate((
+            (enc_hbm, own_rows), (lam_hbm, lam_ref), (q_hbm, q_ref),
+            (tab_hbm, tab_ref), (book_hbm, book_ref),
+        ))
+    ]
+    for copy in loads:
+        copy.start()
+
     barrier = pltpu.get_barrier_semaphore()
 
     def greet(device):
@@ -106,8 +117,9 @@
     def lanes(index, size):
         return pl.ds(pl.multiple_of(index * size, size), size)
 
-    wg[yy, xx, core] = enc_ref[...]
-    over_x(lambda x: small(enc_ref, wg.at[yy, xx, core], AGX, at_x(x)))
+    loads[0].wait()
+    over_x(lambda x: small(own_rows, own_rows, AGX, at_x(x)))
+    loads[1].wait()
     small(lam_ref.at[pl.ds(per_frame, per_frame)], prev, LAM, at_t((me + 1) % nt))
     code_a, code_b = code_ref[0, 0], code_ref[0, 1]
     boundary = start_ref[0]
@@ -133,23 +145,18 @@
         ).start()
 
     scatter_in(1, k_ref, kb, 0)
-    scatter_in(2, v_ref, vb, 0)
+    for copy in loads[2:]:
+        copy.wait()
     table = tab_ref[...]
     code_ids = lax.broadcasted_iota(jnp.int32, table.shape, 0)
     for frame, code in ((0, code_a), (1, code_b)):
         offset = jnp.sum(jnp.where(code_ids == code, table, 0.0), axis=0, keepdims=True)
         span = pl.ds(frame * per_frame, per_frame)
         cond[span] = (q_ref[span].astype(F32) + offset).astype(BF)
-    scatter_in(0, cond, qb, 0)
-    scatter_in(3, g_ref, gb, 0)
-    for head in range(1, heads):
-        scatter_in(1, k_ref, kb, head)
-        scatter_in(0, cond, qb, head)
-        scatter_in(2, v_ref, vb, head)
-        scatter_in(3, g_ref, gb, head)
 
     wait_bytes(wg.at[0, pl.ds(0, nx - 1), 0], small_recv.at[AGX])
     over_y(lambda y: small(wg.at[yy, :, core], wg.at[yy, :, core], AGY, at_y(y)))
+    scatter_in(0, cond, qb, 0)
     wait_bytes(prev, small_recv.at[LAM])
     lam = lam_ref[...].astype(F32)
     before = jnp.where(me > 0, prev[...].astype(F32), 0.0)
@@ -158,6 +165,8 @@
     ).astype(BF)
     wait_bytes(wg.at[pl.ds(0, ny - 1), :, 0], small_recv.at[AGY])
     small(wg.at[:, :, core], wg.at[:, :, core], AGC, other_core)
+    scatter_in(2, v_ref, vb, 0)
+    scatter_in(3, g_ref, gb, 0)
     delta_t = delta.T
     wait_bytes(wg.at[:, :, 0], small_recv.at[AGC])
     slab = lam_width // ny
@@ -224,9 +233,9 @@
         total = rt[0].astype(F32)
         for t in range(1, nt):
             total += rt[t].astype(F32)
-        s4[...] = total.astype(BF).astype(F32)
-        over_t(lambda t: small(s4, ge_out.at[:, lanes(me, part)], GE, at_t(t)))
-        pltpu.make_async_copy(s4, ge_out.at[:, lanes(me, part)], small_recv.at[GE]).start()
+        s4[...] = total.astype(BF)
+        ge[:, lanes(me, part)] = s4[...]
+        over_t(lambda t: small(s4, ge.at[:, lanes(me, part)], GE, at_t(t)))
 
     score_scale = 1.0 / math.sqrt(HS)
     exp_scale = score_scale * math.log2(math.e)
@@ -268,32 +277,52 @@
                 dv_acc[:size] += dv_part
         dkb[head] = dk_acc[...].astype(BF)
         dvb[head] = dv_acc[...].astype(BF)
-        for index, src, dst in ((0, ob, o_out), (1, dqb, dq_out), (2, dkb, dk_out), (3, dvb, dv_out)):
-            columns = lanes(me * heads + head, HS)
-
-            def block(t):
-                return src.at[head, pl.ds(pl.multiple_of(t * here, here), here)]
-
-            over_t(lambda t: send(
-                block(t), dst.at[:, columns], out_send.at[index], out_recv.at[index], at_t(t)
-            ))
-            pltpu.make_async_copy(block(me), dst.at[:, columns], out_recv.at[index]).start()
-
-    def head_step(head, carry):
+
+    outputs = ((ob, o_out), (dqb, dq_out), (dkb, dk_out), (dvb, dv_out))
+
+    def scatter_out(index, head):
+        src, dst = outputs[index]
+        columns = lanes(me * heads + head, HS)
+
+        def block(t):
+            return src.at[head, pl.ds(pl.multiple_of(t * here, here), here)]
+
+        over_t(lambda t: send(
+            block(t), dst.at[:, columns], out_send.at[index], out_recv.at[index], at_t(t)
+        ))
+        pltpu.make_async_copy(block(me), dst.at[:, columns], out_recv.at[index]).start()
+
+    stages = [add_cores, add_y, add_x, add_t]
+    inputs = ((k_ref, kb, 1), (cond, qb, 0), (v_ref, vb, 2), (g_ref, gb, 3))
+    pieces = [(src, dst, index, head) for head in range(1, heads) for src, dst, index in inputs]
+
+    def feed(count):
+        for src, dst, index, head in pieces[:count]:
+            scatter_in(index, src, dst, head)
+        del pieces[:count]
+
+    def advance():
+        if stages:
+            stages.pop(0)()
+
+    feed(2)
+    advance()
+    feed(2)
+    for head in range(heads):
         attend(head)
-
-        @pl.when(head == 0)
-        def _():
-            add_cores()
-
-        @pl.when(head == 1)
-        def _():
-            add_y()
-
-        return carry
-
-    lax.fori_loop(0, heads, head_step, 0)
-    add_x()
+        if head < heads - 1:
+            feed(1)
+            advance()
+            feed(1)
+            scatter_out(0, head)
+            scatter_out(1, head)
+            feed(1)
+            advance()
+            feed(1)
+            scatter_out(2, head)
+            scatter_out(3, head)
+    while stages:
+        advance()
 
     wait_bytes(onehot.at[:, pl.ds(0, (nt - 1) * here)], small_recv.at[HOT])
     hot = onehot[...].astype(BF)
@@ -305,10 +334,12 @@
         total += cin[t]
     blob[:, width:] = total
     small(blob, core_in, ARC, other_core)
-    add_t()
+    scatter_out(0, heads - 1)
+    scatter_out(1, heads - 1)
     wait_bytes(core_in, small_recv.at[ARC])
     y_in[yy] = blob[...] + core_in[...]
     over_y(lambda y: small(y_in.at[yy], y_in.at[yy], ARY, at_y(y)))
+    scatter_out(2, heads - 1)
     wait_bytes(y_in.at[pl.ds(0, ny - 1)], small_recv.at[ARY])
     total = y_in[0]
     for y in range(1, ny):
@@ -327,10 +358,14 @@
     over_t(lambda t: small(book_part, book_dst, FC, at_t(t)))
     pltpu.make_async_copy(act_part, act_dst, small_recv.at[FA]).start()
     pltpu.make_async_copy(book_part, book_dst, small_recv.at[FC]).start()
+    scatter_out(3, heads - 1)
 
     for index, dst in enumerate((o_out, dq_out, dk_out, dv_out)):
         wait_bytes(dst, out_recv.at[index])
-    wait_bytes(ge_out, small_recv.at[GE])
+    wait_bytes(ge.at[:, pl.ds(0, (nt - 1) * part)], small_recv.at[GE])
+    store = pltpu.make_async_copy(ge, ge_out, load.at[0])
+    store.start()
+    store.wait()
     wait_bytes(ga_out, small_recv.at[FA])
     wait_bytes(gc_out, small_recv.at[FC])
     sent = qb.at[:, pl.ds(0, rows - here)]
@@ -347,7 +382,7 @@
         (RSY, ry.at[pl.ds(0, ny - 1)]),
         (RSX, rx.at[pl.ds(0, nx - 1)]),
         (RST, rt.at[pl.ds(0, nt - 1)]),
-        (GE, ge_out.at[:, pl.ds(0, (nt - 1) * part)]),
+        (GE, ge.at[:, pl.ds(0, (nt - 1) * part)]),
         (CT, cin.at[pl.ds(0, nt - 1)]),
         (ARY, y_in.at[pl.ds(0, ny - 1)]),
         (ARX, x_in.at[pl.ds(0, nx - 1)]),
@@ -355,6 +390,24 @@
         (FC, gc_out.at[:, pl.ds(0, (nt - 1) * part)]),
     ):
         wait_bytes(view, small_send.at[index])
+
+
+def keep(*refs):
+    raw, done = refs[:7], refs[7:14]
+    held, sem_in, sem_out = refs[14:21], refs[21], refs[22]
+    loads = [pltpu.make_async_copy(raw[i], held[i], sem_in.at[i]) for i in range(7)]
+    for copy in loads:
+        copy.start()
+    stores = [
+        pltpu.make_async_copy(held[i], done[i], sem_out.at[i]) for i in range(6)
+    ]
+    for i in range(6):
+        loads[i].wait()
+        stores[i].start()
+    loads[6].wait()
+    done[6][...] = held[6][...].astype(F32)
+    for copy in stores:
+        copy.wait()
 
 
 def per_device(
@@ -383,11 +436,15 @@
             flat, flat, flat, flat,
             jax.ShapeDtypeStruct(action_table.shape, F32),
             jax.ShapeDtypeStruct(codebook.shape, F32),
-            jax.ShapeDtypeStruct(enc_weight.shape, F32),
+            jax.ShapeDtypeStruct(enc_weight.shape, BF),
         ),
-        in_specs=[vmem, anywhere, anywhere, anywhere, vmem, vmem, vmem, vmem, smem, smem],
+        in_specs=[anywhere] * 8 + [smem, smem],
         out_specs=[anywhere] * 7,
         scratch_shapes=[
+            pltpu.VMEM((here, wide), BF),
+            pltpu.VMEM(action_table.shape, F32),
+            pltpu.VMEM((here, lam_width), BF),
+            pltpu.VMEM(codebook.shape, F32),
             pltpu.VMEM((here, wide), BF),
             head_block, head_block, head_block, head_block,
             head_block, head_block, head_block, head_block,
@@ -405,13 +462,15 @@
             pltpu.VMEM((nx, enc_rows, lam_width), BF),
             pltpu.VMEM((nt, enc_rows, part), BF),
             pltpu.VMEM((nt, enc_rows, part), BF),
-            pltpu.VMEM((enc_rows, part), F32),
+            pltpu.VMEM((enc_rows, part), BF),
+            pltpu.VMEM((enc_rows, lam_width), BF),
             pltpu.VMEM((nt, NC, part), F32),
             pltpu.VMEM((nt, NC, part), F32),
             pltpu.VMEM((NC, heads * HS + part), F32),
             pltpu.VMEM((NC, heads * HS + part), F32),
             pltpu.VMEM((ny, NC, heads * HS + part), F32),
             pltpu.VMEM((nx, NC, heads * HS + part), F32),
+            pltpu.SemaphoreType.DMA((5,)),
             pltpu.SemaphoreType.DMA((4, heads)),
             pltpu.SemaphoreType.DMA((4,)),
             pltpu.SemaphoreType.DMA((4,)),
@@ -430,6 +489,15 @@
         out_grad.reshape(here, wide), action_table, lam_tokens.reshape(here, lam_width),
         enc_weight, codebook, action_codes, episode_start,
     )
+    results = pl.pallas_call(
+        keep,
+        out_shape=tuple(jax.ShapeDtypeStruct(r.shape, r.dtype) for r in results[:6])
+        + (jax.ShapeDtypeStruct(enc_weight.shape, F32),),
+        in_specs=[anywhere] * 7,
+        out_specs=[anywhere] * 6 + [vmem],
+        scratch_shapes=[pltpu.VMEM(r.shape, r.dtype) for r in results]
+        + [pltpu.SemaphoreType.DMA((7,)), pltpu.SemaphoreType.DMA((6,))],
+    )(*results)
     return tuple(r.reshape(shape) for r in results[:4]) + tuple(results[4:])
 
 

time: 177 us -> 165 us (0.932)
  local copies, waits for them, and re-layouts: 7.96 us -> 0 us
  Pallas kernels: 167 us -> 162 us
    pallas_call x1, Pallas kernels: 167 us -> 158 us  [per_device(): pl.pallas_call(functools.partial(kernel, (ny, nx, nc, nt, chunk)), out_sh...]
    unnamed x19 -> x0, local copies, waits for them, and re-layouts: 7.96 us -> none
    pallas_call x0 -> x1, Pallas kernels: none -> 3.58 us  [per_device(): pl.pallas_call(keep, out_shape=tuple((jax.ShapeDtypeStruct(r.shape, r.dty...]
where the time goes in v2:
time: 165 us; the launch traced here: 163 us
  Pallas kernels  162 us (98%)
    pallas_call x1, Pallas kernels, per_device(): pl.pallas_call(functools.partial(kernel, (ny, nx, nc, nt, chunk)), out_sh...  158 us
    pallas_call x1, Pallas kernels, per_device(): pl.pallas_call(keep, out_shape=tuple((jax.ShapeDtypeStruct(r.shape, r.dty...  3.58 us

profile of v2, /device:TPU:2, one launch (start us, length us, event | category | flops | bytes accessed | tf_op | source)
XLA Modules:
  0.0 163.0 jit_solution(15524001518015041160)
XLA Ops:
  1.3 158.0 %shard_map.153 = (bf16[128,3072]{1,0:T(8,128)(2,1)}, bf16[128,3072]{1,0:T(8,128)(2,1)}, bf16[128,3072]{1,0:T(8,128)(2,1)}, bf16[128,3072]{1,0:T(8,128)(2,1)}, f3...) custom-call(bf16[128,3072]{1,0:T(8,128)(2,1)} %bitcast.9, bf16[128,3072]{1,0:T(8,128)(2,1)} %bitcast.10, ...), custom_call_target="tpu_custom_call" | custom-call | flops 5368709120 | bytes 6291456 | tf_op jit(solution)/shard_map/pallas_call | solution.py:433
  159.2 3.6 %shard_map.154 = (bf16[128,3072]{1,0:T(8,128)(2,1)}, bf16[128,3072]{1,0:T(8,128)(2,1)}, bf16[128,3072]{1,0:T(8,128)(2,1)}, bf16[128,3072]{1,0:T(8,128)(2,1)}, f3...) custom-call(bf16[128,3072]{1,0:T(8,128)(2,1)} %get-tuple-element.21.refs_0_, ...), custom_call_target="tpu_custom_call" | custom-call | tf_op jit(solution)/shard_map/pallas_call | solution.py:492

commit v3 on v2

--- a/solution.py
+++ b/solution.py
@@ -11,6 +11,7 @@
 HS = 128
 NC = 8
 NEG_FILL = -1e30
+ORDER = "iciyiidiieiisiiAoosiioosAoosooAtoototto"
 MESH = pl.DeviceIdType.MESH
 BF = jnp.bfloat16
 F32 = jnp.float32
@@ -29,8 +30,8 @@
     q_hbm, k_ref, v_ref, g_ref, tab_hbm, lam_hbm, enc_hbm, book_hbm, code_ref, start_ref,
     o_out, dq_out, dk_out, dv_out, ga_out, gc_out, ge_out,
     q_ref, tab_ref, lam_ref, book_ref, cond, qb, kb, vb, gb, ob, dqb, dkb, dvb, kt, vt, qt, gt, dk_acc, dv_acc,
-    onehot, prev, wg, dw, rc, s1, ry, s2, rx, s3, rt, s4, ge,
-    cterm, cin, blob, core_in, y_in, x_in,
+    codes, prev, wg, dw, rc, s1, ry, s2, rx, s3, rt, s4, ge,
+    cterm, cin, blob, core_in, y_in, x_in, sums, ga, gc,
     load, in_recv, in_send, out_recv, out_send, small_recv, small_send,
 ):
     ny, nx, nc, nt, chunk = sizes
@@ -109,7 +110,7 @@
             device_id=device, device_id_type=MESH,
         ).start()
 
-    LAM, AGX, AGY, AGC, HOT, RSC, RSY, RSX, RST, GE, CT, ARC, ARY, ARX, FA, FC = range(16)
+    LAM, AGX, AGY, AGC, HOT, RSC, RSY, RSX, RST, GE, CT, ARC, ARY, ARX, FA = range(15)
 
     def small(src, dst, index, device):
         send(src, dst, small_send.at[index], small_recv.at[index], device)
@@ -124,11 +125,10 @@
     code_a, code_b = code_ref[0, 0], code_ref[0, 1]
     boundary = start_ref[0]
     lane_code = jnp.where(
-        lax.broadcasted_iota(jnp.int32, (NC, here), 1) < per_frame, code_a, code_b
+        lax.broadcasted_iota(jnp.int32, (1, here), 1) < per_frame, code_a, code_b
     )
-    hot_here = (lax.broadcasted_iota(jnp.int32, (NC, here), 0) == lane_code).astype(F32)
-    onehot[:, lanes(me, here)] = hot_here
-    over_t(lambda t: small(onehot.at[:, lanes(me, here)], onehot.at[:, lanes(me, here)], HOT, at_t(t)))
+    codes[me] = lane_code.astype(F32)
+    over_t(lambda t: small(codes.at[me], codes.at[me], HOT, at_t(t)))
 
     mine = pl.ds(pl.multiple_of(me * here, here), here)
 
@@ -144,62 +144,65 @@
             src.at[:, lanes(me * heads + head, HS)], dst.at[head, mine], in_recv.at[index, head]
         ).start()
 
-    scatter_in(1, k_ref, kb, 0)
-    for copy in loads[2:]:
-        copy.wait()
-    table = tab_ref[...]
-    code_ids = lax.broadcasted_iota(jnp.int32, table.shape, 0)
-    for frame, code in ((0, code_a), (1, code_b)):
-        offset = jnp.sum(jnp.where(code_ids == code, table, 0.0), axis=0, keepdims=True)
-        span = pl.ds(frame * per_frame, per_frame)
-        cond[span] = (q_ref[span].astype(F32) + offset).astype(BF)
-
-    wait_bytes(wg.at[0, pl.ds(0, nx - 1), 0], small_recv.at[AGX])
-    over_y(lambda y: small(wg.at[yy, :, core], wg.at[yy, :, core], AGY, at_y(y)))
-    scatter_in(0, cond, qb, 0)
-    wait_bytes(prev, small_recv.at[LAM])
-    lam = lam_ref[...].astype(F32)
-    before = jnp.where(me > 0, prev[...].astype(F32), 0.0)
-    delta = jnp.concatenate(
-        [lam[:per_frame] - before, lam[per_frame:] - lam[:per_frame]], axis=0
-    ).astype(BF)
-    wait_bytes(wg.at[pl.ds(0, ny - 1), :, 0], small_recv.at[AGY])
-    small(wg.at[:, :, core], wg.at[:, :, core], AGC, other_core)
-    scatter_in(2, v_ref, vb, 0)
-    scatter_in(3, g_ref, gb, 0)
-    delta_t = delta.T
-    wait_bytes(wg.at[:, :, 0], small_recv.at[AGC])
-    slab = lam_width // ny
-    encoded = jnp.zeros((here, lam_width), F32)
-    for y in range(ny):
-        encoded += dot(delta[:, y * slab:(y + 1) * slab], wg[y].reshape(slab, lam_width))
-    sig = jax.nn.sigmoid(encoded)
-    act = encoded * sig
-    slope = sig * (1.0 + encoded * (1.0 - sig))
-    book = book_ref[...]
-    book_ids = lax.broadcasted_iota(jnp.int32, book.shape, 0)
-    term = jnp.zeros(book.shape, F32)
-    graded = []
-    for frame, code in ((0, code_a), (1, code_b)):
-        span = slice(frame * per_frame, (frame + 1) * per_frame)
-        pooled = jnp.sum(act[span], axis=0, keepdims=True) * (1.0 / per_frame)
-        target = jnp.sum(jnp.where(book_ids == code, book, 0.0), axis=0, keepdims=True)
-        frame_id = me * 2 + frame
-        live = jnp.where((frame_id >= 1) & (frame_id != boundary), 1.0 / (2 * nt), 0.0)
-        residual = (pooled - target) * live
-        term -= jnp.where(book_ids == code, residual, 0.0)
-        graded.append(residual * (1.0 / per_frame) * slope[span])
-    encoded_grad = jnp.concatenate(graded, axis=0).astype(BF)
-    for t in range(nt):
-        cterm[t] = term[:, t * part:(t + 1) * part]
-    cin[me] = cterm[me]
-    over_t(lambda t: small(cterm.at[t], cin.at[me], CT, at_t(t)))
-    for yx in range(ny * nx):
-        lo = yx * nc * enc_rows
-        piece = dot(delta_t[lo:lo + nc * enc_rows], encoded_grad).astype(BF)
-        for c in range(nc):
-            dw[c, yx // nx, yx % nx] = piece[c * enc_rows:(c + 1) * enc_rows]
-    small(dw.at[nc - 1 - core], rc, RSC, other_core)
+    def condition():
+        for copy in loads[2:]:
+            copy.wait()
+        table = tab_ref[...]
+        code_ids = lax.broadcasted_iota(jnp.int32, table.shape, 0)
+        for frame, code in ((0, code_a), (1, code_b)):
+            offset = jnp.sum(jnp.where(code_ids == code, table, 0.0), axis=0, keepdims=True)
+            span = pl.ds(frame * per_frame, per_frame)
+            cond[span] = (q_ref[span].astype(F32) + offset).astype(BF)
+
+    def rows_over_y():
+        wait_bytes(wg.at[0, pl.ds(0, nx - 1), 0], small_recv.at[AGX])
+        over_y(lambda y: small(wg.at[yy, :, core], wg.at[yy, :, core], AGY, at_y(y)))
+
+    def rows_over_cores():
+        wait_bytes(prev, small_recv.at[LAM])
+        lam = lam_ref[...].astype(F32)
+        before = jnp.where(me > 0, prev[...].astype(F32), 0.0)
+        delta = jnp.concatenate(
+            [lam[:per_frame] - before, lam[per_frame:] - lam[:per_frame]], axis=0
+        ).astype(BF)
+        wait_bytes(wg.at[pl.ds(0, ny - 1), :, 0], small_recv.at[AGY])
+        small(wg.at[:, :, core], wg.at[:, :, core], AGC, other_core)
+        return delta
+
+    def encode(delta):
+        delta_t = delta.T
+        wait_bytes(wg.at[:, :, 0], small_recv.at[AGC])
+        slab = lam_width // ny
+        encoded = jnp.zeros((here, lam_width), F32)
+        for y in range(ny):
+            encoded += dot(delta[:, y * slab:(y + 1) * slab], wg[y].reshape(slab, lam_width))
+        sig = jax.nn.sigmoid(encoded)
+        act = encoded * sig
+        slope = sig * (1.0 + encoded * (1.0 - sig))
+        book = book_ref[...]
+        book_ids = lax.broadcasted_iota(jnp.int32, book.shape, 0)
+        term = jnp.zeros(book.shape, F32)
+        graded = []
+        for frame, code in ((0, code_a), (1, code_b)):
+            span = slice(frame * per_frame, (frame + 1) * per_frame)
+            pooled = jnp.sum(act[span], axis=0, keepdims=True) * (1.0 / per_frame)
+            target = jnp.sum(jnp.where(book_ids == code, book, 0.0), axis=0, keepdims=True)
+            frame_id = me * 2 + frame
+            live = jnp.where((frame_id >= 1) & (frame_id != boundary), 1.0 / (2 * nt), 0.0)
+            residual = (pooled - target) * live
+            term -= jnp.where(book_ids == code, residual, 0.0)
+            graded.append(residual * (1.0 / per_frame) * slope[span])
+        encoded_grad = jnp.concatenate(graded, axis=0).astype(BF)
+        for t in range(nt):
+            cterm[t] = term[:, t * part:(t + 1) * part]
+        cin[me] = cterm[me]
+        over_t(lambda t: small(cterm.at[t], cin.at[me], CT, at_t(t)))
+        for yx in range(ny * nx):
+            lo = yx * nc * enc_rows
+            piece = dot(delta_t[lo:lo + nc * enc_rows], encoded_grad).astype(BF)
+            for c in range(nc):
+                dw[c, yx // nx, yx % nx] = piece[c * enc_rows:(c + 1) * enc_rows]
+        small(dw.at[nc - 1 - core], rc, RSC, other_core)
 
     def add_cores():
         wait_bytes(rc, small_recv.at[RSC])
@@ -292,82 +295,86 @@
         ))
         pltpu.make_async_copy(block(me), dst.at[:, columns], out_recv.at[index]).start()
 
-    stages = [add_cores, add_y, add_x, add_t]
+    def sum_over_cores():
+        wait_bytes(codes.at[pl.ds(0, nt - 1)], small_recv.at[HOT])
+        all_codes = jnp.concatenate([codes[t] for t in range(nt)], axis=1)
+        code_rows = lax.broadcasted_iota(jnp.int32, (NC, rows), 0).astype(F32)
+        hot = (code_rows == all_codes).astype(BF)
+        for head in range(heads):
+            blob[:, head * HS:(head + 1) * HS] = dot(hot, dqb[head])
+        wait_bytes(cin.at[pl.ds(0, nt - 1)], small_recv.at[CT])
+        total = cin[0]
+        for t in range(1, nt):
+            total += cin[t]
+        blob[:, width:] = total
+        small(blob, core_in, ARC, other_core)
+
+    def sum_over_y():
+        wait_bytes(core_in, small_recv.at[ARC])
+        y_in[yy] = blob[...] + core_in[...]
+        over_y(lambda y: small(y_in.at[yy], y_in.at[yy], ARY, at_y(y)))
+
+    def sum_over_x():
+        wait_bytes(y_in.at[pl.ds(0, ny - 1)], small_recv.at[ARY])
+        total = y_in[0]
+        for y in range(1, ny):
+            total += y_in[y]
+        x_in[xx] = total
+        over_x(lambda x: small(x_in.at[xx], x_in.at[xx], ARX, at_x(x)))
+
+    def share_sums():
+        wait_bytes(x_in.at[pl.ds(0, nx - 1)], small_recv.at[ARX])
+        total = x_in[0]
+        for x in range(1, nx):
+            total += x_in[x]
+        half = (width + part) // 2
+        sums[me] = jnp.concatenate([total[:, :half], total[:, half:]], axis=0).astype(BF)
+        over_t(lambda t: small(sums.at[me], sums.at[me], FA, at_t(t)))
+
     inputs = ((k_ref, kb, 1), (cond, qb, 0), (v_ref, vb, 2), (g_ref, gb, 3))
-    pieces = [(src, dst, index, head) for head in range(1, heads) for src, dst, index in inputs]
-
-    def feed(count):
-        for src, dst, index, head in pieces[:count]:
-            scatter_in(index, src, dst, head)
-        del pieces[:count]
-
-    def advance():
-        if stages:
-            stages.pop(0)()
-
-    feed(2)
-    advance()
-    feed(2)
-    for head in range(heads):
-        attend(head)
-        if head < heads - 1:
-            feed(1)
-            advance()
-            feed(1)
-            scatter_out(0, head)
-            scatter_out(1, head)
-            feed(1)
-            advance()
-            feed(1)
-            scatter_out(2, head)
-            scatter_out(3, head)
-    while stages:
-        advance()
-
-    wait_bytes(onehot.at[:, pl.ds(0, (nt - 1) * here)], small_recv.at[HOT])
-    hot = onehot[...].astype(BF)
-    for head in range(heads):
-        blob[:, head * HS:(head + 1) * HS] = dot(hot, dqb[head])
-    wait_bytes(cin.at[pl.ds(0, nt - 1)], small_recv.at[CT])
-    total = cin[0]
-    for t in range(1, nt):
-        total += cin[t]
-    blob[:, width:] = total
-    small(blob, core_in, ARC, other_core)
-    scatter_out(0, heads - 1)
-    scatter_out(1, heads - 1)
-    wait_bytes(core_in, small_recv.at[ARC])
-    y_in[yy] = blob[...] + core_in[...]
-    over_y(lambda y: small(y_in.at[yy], y_in.at[yy], ARY, at_y(y)))
-    scatter_out(2, heads - 1)
-    wait_bytes(y_in.at[pl.ds(0, ny - 1)], small_recv.at[ARY])
-    total = y_in[0]
-    for y in range(1, ny):
-        total += y_in[y]
-    x_in[xx] = total
-    over_x(lambda x: small(x_in.at[xx], x_in.at[xx], ARX, at_x(x)))
-    wait_bytes(x_in.at[pl.ds(0, nx - 1)], small_recv.at[ARX])
-    total = x_in[0]
-    for x in range(1, nx):
-        total += x_in[x]
-    wait_bytes(blob, small_send.at[ARC])
-    blob[...] = total
-    act_part, book_part = blob.at[:, pl.ds(0, width)], blob.at[:, pl.ds(width, part)]
-    act_dst, book_dst = ga_out.at[:, lanes(me, width)], gc_out.at[:, lanes(me, part)]
-    over_t(lambda t: small(act_part, act_dst, FA, at_t(t)))
-    over_t(lambda t: small(book_part, book_dst, FC, at_t(t)))
-    pltpu.make_async_copy(act_part, act_dst, small_recv.at[FA]).start()
-    pltpu.make_async_copy(book_part, book_dst, small_recv.at[FC]).start()
-    scatter_out(3, heads - 1)
+    pieces = [(index, src, dst, head) for head in range(heads) for src, dst, index in inputs]
+    results = [(index, head) for head in range(heads) for index in range(4)]
+    steps = {
+        "c": [condition], "y": [rows_over_y], "d": [rows_over_cores],
+        "s": [add_cores, add_y, add_x, add_t],
+        "t": [sum_over_cores, sum_over_y, sum_over_x, share_sums],
+    }
+    done = 0
+    for step in ORDER:
+        if step == "i":
+            if pieces:
+                scatter_in(*pieces.pop(0))
+        elif step == "o":
+            if results:
+                scatter_out(*results.pop(0))
+        elif step == "A":
+            if done < heads:
+                attend(done)
+            done += 1
+        elif step == "d":
+            delta = rows_over_cores()
+        elif step == "e":
+            encode(delta)
+        else:
+            steps[step].pop(0)()
 
     for index, dst in enumerate((o_out, dq_out, dk_out, dv_out)):
         wait_bytes(dst, out_recv.at[index])
     wait_bytes(ge.at[:, pl.ds(0, (nt - 1) * part)], small_recv.at[GE])
-    store = pltpu.make_async_copy(ge, ge_out, load.at[0])
-    store.start()
-    store.wait()
-    wait_bytes(ga_out, small_recv.at[FA])
-    wait_bytes(gc_out, small_recv.at[FC])
+    wait_bytes(sums.at[pl.ds(0, nt - 1)], small_recv.at[FA])
+    for t in range(nt):
+        got = sums[t].astype(F32)
+        got = jnp.concatenate([got[:NC], got[NC:]], axis=1)
+        ga[:, t * width:(t + 1) * width] = got[:, :width]
+        gc[:, t * part:(t + 1) * part] = got[:, width:]
+    ends = [
+        pltpu.make_async_copy(src, dst, load.at[i])
+        for i, (src, dst) in enumerate(((ge, ge_out), (ga, ga_out), (gc, gc_out)))
+    ]
+    for copy in ends:
+        copy.start()
+    for copy in ends:
+        copy.wait()
     sent = qb.at[:, pl.ds(0, rows - here)]
     for index in range(4):
         wait_bytes(sent, in_send.at[index])
@@ -377,8 +384,9 @@
         (AGX, wg.at[0, pl.ds(0, nx - 1), 0]),
         (AGY, wg.at[pl.ds(0, ny - 1), :, 0]),
         (AGC, wg.at[:, :, 0]),
-        (HOT, onehot.at[:, pl.ds(0, (nt - 1) * here)]),
+        (HOT, codes.at[pl.ds(0, nt - 1)]),
         (RSC, rc),
+        (ARC, core_in),
         (RSY, ry.at[pl.ds(0, ny - 1)]),
         (RSX, rx.at[pl.ds(0, nx - 1)]),
         (RST, rt.at[pl.ds(0, nt - 1)]),
@@ -386,28 +394,40 @@
         (CT, cin.at[pl.ds(0, nt - 1)]),
         (ARY, y_in.at[pl.ds(0, ny - 1)]),
         (ARX, x_in.at[pl.ds(0, nx - 1)]),
-        (FA, ga_out.at[:, pl.ds(0, (nt - 1) * width)]),
-        (FC, gc_out.at[:, pl.ds(0, (nt - 1) * part)]),
+        (FA, sums.at[pl.ds(0, nt - 1)]),
     ):
         wait_bytes(view, small_send.at[index])
 
 
-def keep(*refs):
+def keep(pieces, *refs):
     raw, done = refs[:7], refs[7:14]
     held, sem_in, sem_out = refs[14:21], refs[21], refs[22]
-    loads = [pltpu.make_async_copy(raw[i], held[i], sem_in.at[i]) for i in range(7)]
-    for copy in loads:
-        copy.start()
-    stores = [
-        pltpu.make_async_copy(held[i], done[i], sem_out.at[i]) for i in range(6)
-    ]
-    for i in range(6):
-        loads[i].wait()
-        stores[i].start()
-    loads[6].wait()
-    done[6][...] = held[6][...].astype(F32)
-    for copy in stores:
-        copy.wait()
+    loads, stores = [], []
+    for piece in range(pieces):
+        for i in range(7):
+            whole = raw[i].shape[0]
+            rows = whole // pieces if i < 4 else whole
+            if i >= 4 and piece:
+                continue
+            span = pl.ds(piece * rows, rows)
+            loads.append(pltpu.make_async_copy(
+                raw[i].at[span], held[i].at[span], sem_in.at[i, piece]))
+            if i < 6:
+                stores.append(pltpu.make_async_copy(
+                    held[i].at[span], done[i].at[span], sem_out.at[i, piece]))
+            else:
+                stores.append(None)
+    for load in loads:
+        load.start()
+    for load, store in zip(loads, stores):
+        load.wait()
+        if store is None:
+            done[6][...] = held[6][...].astype(F32)
+        else:
+            store.start()
+    for store in stores:
+        if store is not None:
+            store.wait()
 
 
 def per_device(
@@ -451,7 +471,7 @@
             turned, turned, turned, turned,
             pltpu.VMEM((rows, HS), F32),
             pltpu.VMEM((rows, HS), F32),
-            pltpu.VMEM((NC, rows), F32),
+            pltpu.VMEM((nt, 1, here), F32),
             pltpu.VMEM((here // 2, lam_width), BF),
             pltpu.VMEM((ny, nx, nc, enc_rows, lam_width), BF),
             pltpu.VMEM((nc, ny, nx, enc_rows, lam_width), BF),
@@ -470,6 +490,9 @@
             pltpu.VMEM((NC, heads * HS + part), F32),
             pltpu.VMEM((ny, NC, heads * HS + part), F32),
             pltpu.VMEM((nx, NC, heads * HS + part), F32),
+            pltpu.VMEM((nt, 2 * NC, (heads * HS + part) // 2), BF),
+            pltpu.VMEM(action_table.shape, F32),
+            pltpu.VMEM(codebook.shape, F32),
             pltpu.SemaphoreType.DMA((5,)),
             pltpu.SemaphoreType.DMA((4, heads)),
             pltpu.SemaphoreType.DMA((4,)),
@@ -490,13 +513,13 @@
         enc_weight, codebook, action_codes, episode_start,
     )
     results = pl.pallas_call(
-        keep,
+        functools.partial(keep, 1),
         out_shape=tuple(jax.ShapeDtypeStruct(r.shape, r.dtype) for r in results[:6])
         + (jax.ShapeDtypeStruct(enc_weight.shape, F32),),
         in_specs=[anywhere] * 7,
         out_specs=[anywhere] * 6 + [vmem],
         scratch_shapes=[pltpu.VMEM(r.shape, r.dtype) for r in results]
-        + [pltpu.SemaphoreType.DMA((7,)), pltpu.SemaphoreType.DMA((6,))],
+        + [pltpu.SemaphoreType.DMA((7, 1)), pltpu.SemaphoreType.DMA((6, 1))],
     )(*results)
     return tuple(r.reshape(shape) for r in results[:4]) + tuple(results[4:])
 

time: 165 us -> 160 us (0.970)
  Pallas kernels: 162 us -> 158 us
    pallas_call x1, Pallas kernels: 158 us -> 155 us  [per_device(): pl.pallas_call(functools.partial(kernel, (ny, nx, nc, nt, chunk)), out_sh...]
where the time goes in v3:
time: 160 us
  Pallas kernels  158 us (99%)
    pallas_call x1, Pallas kernels, per_device(): pl.pallas_call(functools.partial(kernel, (ny, nx, nc, nt, chunk)), out_sh...  155 us
    pallas_call x1, Pallas kernels, per_device(): pl.pallas_call(functools.partial(keep, 1), out_shape=tuple((jax.ShapeDtyp...  3.58 us

profile of v3, /device:TPU:2, one launch (start us, length us, event | category | flops | bytes accessed | tf_op | source)
XLA Modules:
  0.0 159.6 jit_solution(5669091794934190099)
XLA Ops:
  1.3 154.6 %shard_map.153 = (bf16[128,3072]{1,0:T(8,128)(2,1)}, bf16[128,3072]{1,0:T(8,128)(2,1)}, bf16[128,3072]{1,0:T(8,128)(2,1)}, bf16[128,3072]{1,0:T(8,128)(2,1)}, f3...) custom-call(bf16[128,3072]{1,0:T(8,128)(2,1)} %bitcast.9, bf16[128,3072]{1,0:T(8,128)(2,1)} %bitcast.10, ...), custom_call_target="tpu_custom_call" | custom-call | flops 5368709120 | bytes 6291456 | tf_op jit(solution)/shard_map/pallas_call | solution.py:453
  155.9 3.6 %shard_map.154 = (bf16[128,3072]{1,0:T(8,128)(2,1)}, bf16[128,3072]{1,0:T(8,128)(2,1)}, bf16[128,3072]{1,0:T(8,128)(2,1)}, bf16[128,3072]{1,0:T(8,128)(2,1)}, f3...) custom-call(bf16[128,3072]{1,0:T(8,128)(2,1)} %get-tuple-element.21.refs_0_, ...), custom_call_target="tpu_custom_call" | custom-call | tf_op jit(solution)/shard_map/pallas_call | solution.py:515

commit v4 on v3

--- a/solution.py
+++ b/solution.py
@@ -358,8 +358,6 @@
         else:
             steps[step].pop(0)()
 
-    for index, dst in enumerate((o_out, dq_out, dk_out, dv_out)):
-        wait_bytes(dst, out_recv.at[index])
     wait_bytes(ge.at[:, pl.ds(0, (nt - 1) * part)], small_recv.at[GE])
     wait_bytes(sums.at[pl.ds(0, nt - 1)], small_recv.at[FA])
     for t in range(nt):
@@ -373,8 +371,8 @@
     ]
     for copy in ends:
         copy.start()
-    for copy in ends:
-        copy.wait()
+    for index, dst in enumerate((o_out, dq_out, dk_out, dv_out)):
+        wait_bytes(dst, out_recv.at[index])
     sent = qb.at[:, pl.ds(0, rows - here)]
     for index in range(4):
         wait_bytes(sent, in_send.at[index])
@@ -397,37 +395,21 @@
         (FA, sums.at[pl.ds(0, nt - 1)]),
     ):
         wait_bytes(view, small_send.at[index])
-
-
-def keep(pieces, *refs):
-    raw, done = refs[:7], refs[7:14]
-    held, sem_in, sem_out = refs[14:21], refs[21], refs[22]
-    loads, stores = [], []
-    for piece in range(pieces):
-        for i in range(7):
-            whole = raw[i].shape[0]
-            rows = whole // pieces if i < 4 else whole
-            if i >= 4 and piece:
-                continue
-            span = pl.ds(piece * rows, rows)
-            loads.append(pltpu.make_async_copy(
-                raw[i].at[span], held[i].at[span], sem_in.at[i, piece]))
-            if i < 6:
-                stores.append(pltpu.make_async_copy(
-                    held[i].at[span], done[i].at[span], sem_out.at[i, piece]))
-            else:
-                stores.append(None)
-    for load in loads:
-        load.start()
-    for load, store in zip(loads, stores):
-        load.wait()
-        if store is None:
-            done[6][...] = held[6][...].astype(F32)
-        else:
-            store.start()
-    for store in stores:
-        if store is not None:
-            store.wait()
+    for copy in ends:
+        copy.wait()
+
+
+def keep(*refs):
+    raw, done, held, sem_in, sem_out = refs[:7], refs[7:14], *refs[14:]
+    stores = [pltpu.make_async_copy(raw[i], done[i], sem_out.at[i]) for i in range(6)]
+    load = pltpu.make_async_copy(raw[6], held, sem_in)
+    load.start()
+    for copy in stores:
+        copy.start()
+    load.wait()
+    done[6][...] = held[...].astype(F32)
+    for copy in stores:
+        copy.wait()
 
 
 def per_device(
@@ -502,24 +484,34 @@
             pltpu.SemaphoreType.DMA((16,)),
         ],
         compiler_params=pltpu.CompilerParams(
-            collective_id=0, has_side_effects=True, vmem_limit_bytes=56 * 2**20
+            collective_id=0, has_side_effects=True, vmem_limit_bytes=32 * 2**20
         ),
         cost_estimate=pl.CostEstimate(
             flops=flops, bytes_accessed=8 * here * wide * 2, transcendentals=heads * rows * rows
         ),
     )(
-        queries.reshape(here, wide), keys.reshape(here, wide), values.reshape(here, wide),
-        out_grad.reshape(here, wide), action_table, lam_tokens.reshape(here, lam_width),
-        enc_weight, codebook, action_codes, episode_start,
+        *(
+            pltpu.with_memory_space_constraint(x, pltpu.HBM)
+            for x in (
+                queries.reshape(here, wide), keys.reshape(here, wide), values.reshape(here, wide),
+                out_grad.reshape(here, wide), action_table, lam_tokens.reshape(here, lam_width),
+                enc_weight, codebook,
+            )
+        ),
+        action_codes, episode_start,
     )
     results = pl.pallas_call(
-        functools.partial(keep, 1),
+        keep,
         out_shape=tuple(jax.ShapeDtypeStruct(r.shape, r.dtype) for r in results[:6])
         + (jax.ShapeDtypeStruct(enc_weight.shape, F32),),
         in_specs=[anywhere] * 7,
         out_specs=[anywhere] * 6 + [vmem],
-        scratch_shapes=[pltpu.VMEM(r.shape, r.dtype) for r in results]
-        + [pltpu.SemaphoreType.DMA((7, 1)), pltpu.SemaphoreType.DMA((6, 1))],
+        compiler_params=pltpu.CompilerParams(vmem_limit_bytes=8 * 2**20),
+        scratch_shapes=[
+            pltpu.VMEM(enc_weight.shape, BF),
+            pltpu.SemaphoreType.DMA,
+            pltpu.SemaphoreType.DMA((6,)),
+        ],
     )(*results)
     return tuple(r.reshape(shape) for r in results[:4]) + tuple(results[4:])
 

time: 160 us -> 158 us (0.988)
  Pallas kernels: 158 us -> 156 us
where the time goes in v4:
time: 158 us
  Pallas kernels  156 us (99%)
    pallas_call x1, Pallas kernels, per_device(): pl.pallas_call(functools.partial(kernel, (ny, nx, nc, nt, chunk)), out_sh...  154 us

profile of v4, /device:TPU:2, one launch (start us, length us, event | category | flops | bytes accessed | tf_op | source)
XLA Modules:
  0.0 158.1 jit_solution(12015061313784651630)
XLA Ops:
  1.3 0.0 copy-start
  1.3 0.6 copy-done
  1.9 153.5 %shard_map.153 = (bf16[128,3072]{1,0:T(8,128)(2,1)S(1)}, bf16[128,3072]{1,0:T(8,128)(2,1)S(1)}, bf16[128,3072]{1,0:T(8,128)(2,1)S(1)}, bf16[128,3072]{1,0:T(8,12...) custom-call(bf16[128,3072]{1,0:T(8,128)(2,1)} %bitcast.9, ...), custom_call_target="tpu_custom_call" | custom-call | flops 5368709120 | bytes 6291456 | tf_op jit(solution)/shard_map/pallas_call | solution.py:435
  155.5 2.5 %shard_map.154 = (bf16[128,3072]{1,0:T(8,128)(2,1)}, bf16[128,3072]{1,0:T(8,128)(2,1)}, bf16[128,3072]{1,0:T(8,128)(2,1)}, bf16[128,3072]{1,0:T(8,128)(2,1)}, f3...) custom-call(bf16[128,3072]{1,0:T(8,128)(2,1)S(1)} %get-tuple-element.21.refs_0_, ...), custom_call_target="tpu_custom_call" | custom-call | tf_op jit(solution)/shard_map/pallas_call | solution.py:503
Async XLA Ops:
  1.3 0.7 copy-start

commit v5 on v4

--- a/solution.py
+++ b/solution.py
@@ -27,9 +27,9 @@
 
 def kernel(
     sizes,
-    q_hbm, k_ref, v_ref, g_ref, tab_hbm, lam_hbm, enc_hbm, book_hbm, code_ref, start_ref,
+    q_hbm, k_ref, v_ref, g_ref, tab_hbm, lam_hbm, enc_hbm, book_hbm, code_hbm, start_ref,
     o_out, dq_out, dk_out, dv_out, ga_out, gc_out, ge_out,
-    q_ref, tab_ref, lam_ref, book_ref, cond, qb, kb, vb, gb, ob, dqb, dkb, dvb, kt, vt, qt, gt, dk_acc, dv_acc,
+    code_ref, q_ref, tab_ref, lam_ref, book_ref, cond, qb, kb, vb, gb, ob, dqb, dkb, dvb, kt, vt, qt, gt, dk_acc, dv_acc,
     codes, prev, wg, dw, rc, s1, ry, s2, rx, s3, rt, s4, ge,
     cterm, cin, blob, core_in, y_in, x_in, sums, ga, gc,
     load, in_recv, in_send, out_recv, out_send, small_recv, small_send,
@@ -87,7 +87,7 @@
         pltpu.make_async_copy(src, dst, load.at[i])
         for i, (src, dst) in enumerate((
             (enc_hbm, own_rows), (lam_hbm, lam_ref), (q_hbm, q_ref),
-            (tab_hbm, tab_ref), (book_hbm, book_ref),
+            (tab_hbm, tab_ref), (book_hbm, book_ref), (code_hbm, code_ref),
         ))
     ]
     for copy in loads:
@@ -121,6 +121,7 @@
     loads[0].wait()
     over_x(lambda x: small(own_rows, own_rows, AGX, at_x(x)))
     loads[1].wait()
+    loads[5].wait()
     small(lam_ref.at[pl.ds(per_frame, per_frame)], prev, LAM, at_t((me + 1) % nt))
     code_a, code_b = code_ref[0, 0], code_ref[0, 1]
     boundary = start_ref[0]
@@ -145,7 +146,7 @@
         ).start()
 
     def condition():
-        for copy in loads[2:]:
+        for copy in loads[2:5]:
             copy.wait()
         table = tab_ref[...]
         code_ids = lax.broadcasted_iota(jnp.int32, table.shape, 0)
@@ -440,9 +441,10 @@
             jax.ShapeDtypeStruct(codebook.shape, F32),
             jax.ShapeDtypeStruct(enc_weight.shape, BF),
         ),
-        in_specs=[anywhere] * 8 + [smem, smem],
+        in_specs=[anywhere] * 9 + [smem],
         out_specs=[anywhere] * 7,
         scratch_shapes=[
+            pltpu.SMEM(action_codes.shape, jnp.int32),
             pltpu.VMEM((here, wide), BF),
             pltpu.VMEM(action_table.shape, F32),
             pltpu.VMEM((here, lam_width), BF),
@@ -475,7 +477,7 @@
             pltpu.VMEM((nt, 2 * NC, (heads * HS + part) // 2), BF),
             pltpu.VMEM(action_table.shape, F32),
             pltpu.VMEM(codebook.shape, F32),
-            pltpu.SemaphoreType.DMA((5,)),
+            pltpu.SemaphoreType.DMA((6,)),
             pltpu.SemaphoreType.DMA((4, heads)),
             pltpu.SemaphoreType.DMA((4,)),
             pltpu.SemaphoreType.DMA((4,)),
@@ -495,10 +497,10 @@
             for x in (
                 queries.reshape(here, wide), keys.reshape(here, wide), values.reshape(here, wide),
                 out_grad.reshape(here, wide), action_table, lam_tokens.reshape(here, lam_width),
-                enc_weight, codebook,
+                enc_weight, codebook, action_codes,
             )
         ),
-        action_codes, episode_start,
+        episode_start,
     )
     results = pl.pallas_call(
         keep,

time: 158 us -> 157 us (level)
  no operation moved by 1% of the time
where the time goes in v5:
time: 157 us
  Pallas kernels  156 us (99%)
    pallas_call x1, Pallas kernels, per_device(): pl.pallas_call(functools.partial(kernel, (ny, nx, nc, nt, chunk)), out_sh...  153 us

profile of v5, /device:TPU:2, one launch (start us, length us, event | category | flops | bytes accessed | tf_op | source)
XLA Modules:
  0.0 157.1 jit_solution(13580973381297977226)
XLA Ops:
  1.3 153.2 %shard_map.153 = (bf16[128,3072]{1,0:T(8,128)(2,1)S(1)}, bf16[128,3072]{1,0:T(8,128)(2,1)S(1)}, bf16[128,3072]{1,0:T(8,128)(2,1)S(1)}, bf16[128,3072]{1,0:T(8,12...) custom-call(bf16[128,3072]{1,0:T(8,128)(2,1)} %bitcast.9, ...), custom_call_target="tpu_custom_call" | custom-call | flops 5368709120 | bytes 6291456 | tf_op jit(solution)/shard_map/pallas_call | solution.py:436
  154.4 2.5 %shard_map.154 = (bf16[128,3072]{1,0:T(8,128)(2,1)}, bf16[128,3072]{1,0:T(8,128)(2,1)}, bf16[128,3072]{1,0:T(8,128)(2,1)}, bf16[128,3072]{1,0:T(8,128)(2,1)}, f3...) custom-call(bf16[128,3072]{1,0:T(8,128)(2,1)S(1)} %get-tuple-element.21.refs_0_, ...), custom_call_target="tpu_custom_call" | custom-call | tf_op jit(solution)/shard_map/pallas_call | solution.py:505
